TPU v7x, 512 devices: a whole 4x4x16 slice. The times are simulated.
512 devices in a mesh: sub: 64 (over z_lo, y, core), strip: 8 (over x, z_hi).
Axes of the slice: x: 4, y: 4, z: 16 (z_hi: 2, z_lo: 8; z = z_hi * 8 + z_lo), core: 2. Of those that a mesh axis runs over, the one named last changes fastest.
Arguments:
- spectra: bfloat16 [128, 256, 2048], P('sub', 'strip'), may hold values from -6 to 6
- offsets: int32 [128], P('sub'), may hold values from 0 to 1023
Outputs:
- foreground: float32 [1024, 256, 128], P('strip', 'sub')
All inputs are finite; a program needn't handle non-finite values.
Results may differ from a plain program's by a relative error of at most 0.0068.
Values may be sent and summed in bfloat16 or wider, within the bound.
No kernel may reach another device: no remote copies, remote signals or barrier semaphores. Data moves between devices by JAX's collectives and lax.ppermute only.
A program may use at most 64 MiB of HBM per device.

v0:
```python
import math

import jax
import jax.numpy as jnp
import numpy as np
from jax import lax
from jax.sharding import PartitionSpec as P

KR = 256
ROWS = 1024
COLS = 256
WIN = 8
BG = 16


def from_behind(value, axis, steps):
    count = lax.axis_size(axis)
    pairs = [(source, (source + steps) % count) for source in range(count)]
    return lax.ppermute(value, axis, pairs)


def extended(shard, sides, width):
    for axis, dim in sides:
        count, length = (lax.axis_size(axis), shard.shape[dim])
        up = [(i, (i + 1) % count) for i in range(count - 1)]
        down = [(j, i) for i, j in up]
        last = lax.slice_in_dim(shard, length - width, length, axis=dim)
        leading = lax.slice_in_dim(shard, 0, width, axis=dim)
        before = lax.ppermute(last, axis, up)
        after = lax.ppermute(leading, axis, down)
        shard = jnp.concatenate([before, shard, after], axis=dim)
    return shard


def column_table(samples, width):
    sample_index = jnp.arange(samples, dtype=jnp.int32)[:, None]
    column_index = jnp.arange(width, dtype=jnp.int32)[None, :]
    phase = jnp.mod(sample_index * column_index, samples).astype(jnp.float32) * (
        2.0 * math.pi / samples
    )
    cosine = jnp.cos(phase) / math.sqrt(samples)
    sine = -jnp.sin(phase) / math.sqrt(samples)
    upper = jnp.concatenate([cosine, sine], axis=1)
    lower = jnp.concatenate([-sine, cosine], axis=1)
    return jnp.concatenate([upper, lower], axis=0).astype(jnp.bfloat16)


def row_table(row_index, samples, image_rows):
    sample_index = jnp.arange(samples, dtype=jnp.int32)[None, :] - samples // 2
    phase = jnp.mod(row_index[:, None] * sample_index, image_rows).astype(jnp.float32) * (
        2.0 * math.pi / image_rows
    )
    scale = 1.0 / math.sqrt(samples)
    return jnp.concatenate([jnp.cos(phase) * scale, jnp.sin(phase) * scale], axis=0).astype(
        jnp.bfloat16
    )


def apply_phase(mixed, offsets, sample_index):
    angle = jnp.mod(offsets[:, None] * (sample_index[None, :] - KR // 2), ROWS).astype(
        jnp.float32
    ) * (2.0 * math.pi / ROWS)
    cosine = jnp.cos(angle)[:, :, None]
    sine = jnp.sin(angle)[:, :, None]
    real_part = mixed[:, :, :COLS]
    imag_part = mixed[:, :, COLS:]
    return jnp.concatenate(
        [real_part * cosine - imag_part * sine, real_part * sine + imag_part * cosine], axis=2
    ).astype(jnp.bfloat16)


def window_mask(block_offset, count):
    target = np.arange(count)[:, None]
    source = np.arange(count)[None, :]
    distance = block_offset * count + source - target
    return ((distance >= 0) & (distance < WIN)).astype(np.float32)


def combine_parts(product, strip_rows):
    product = lax.optimization_barrier(product)
    real_part = product[:, :strip_rows, :COLS] - product[:, strip_rows:, COLS:]
    imag_part = product[:, :strip_rows, COLS:] + product[:, strip_rows:, :COLS]
    return jnp.concatenate([real_part, imag_part], axis=2)


def remove_background(stack):
    frame_count = stack.shape[0]
    series = jnp.transpose(stack, (1, 2, 0))
    source = jnp.arange(frame_count, dtype=jnp.int32)[:, None]
    target = jnp.arange(frame_count, dtype=jnp.int32)[None, :]
    behind = jnp.where(jnp.mod(target - source, frame_count) < BG, 1.0 / BG, 0.0).astype(
        jnp.float32
    )
    weights = jnp.where(source == target, 1.0, 0.0).astype(jnp.float32) - behind
    return jnp.einsum("rcg,gf->rcf", series, weights, precision=lax.Precision.HIGHEST)


def body(spectra, offsets):
    sub_dev = spectra.shape[0]
    strip_rows = ROWS // lax.axis_size("strip")
    first_row = lax.axis_index("strip") * strip_rows
    own_rows = first_row + jnp.arange(strip_rows, dtype=jnp.int32)
    columns = column_table(spectra.shape[2] // 2, COLS)
    table = row_table(own_rows, KR, ROWS)
    passes = (WIN - 2 + sub_dev) // sub_dev
    piece = lax.all_gather(spectra, "strip", axis=1, tiled=True)
    sample_index = jnp.arange(piece.shape[1], dtype=jnp.int32)
    shifted = apply_phase(
        jnp.einsum("skc,cn->skn", piece, columns, preferred_element_type=jnp.float32),
        offsets,
        sample_index,
    )
    product = jnp.einsum("mk,skn->smn", table, shifted, preferred_element_type=jnp.float32)
    images = combine_parts(product, strip_rows)
    frames = jnp.einsum(
        "ab,bmn->amn", jnp.asarray(window_mask(0, sub_dev)), images, precision=lax.Precision.HIGHEST
    )
    moving = images
    for block_offset in range(1, passes + 1):
        moving = from_behind(moving, "sub", -1)
        frames = frames + jnp.einsum(
            "ab,bmn->amn",
            jnp.asarray(window_mask(block_offset, sub_dev)),
            moving,
            precision=lax.Precision.HIGHEST,
        )
    real_part = frames[:, :, :COLS]
    imag_part = frames[:, :, COLS:]
    log_power = jnp.log(1.0 + real_part * real_part + imag_part * imag_part)
    padded = extended(log_power, (("strip", 1),), 1)
    padded = jnp.pad(padded, ((0, 0), (0, 0), (1, 1)))
    total = jnp.zeros_like(log_power)
    for row_step in range(3):
        for col_step in range(3):
            total = total + padded[:, row_step : row_step + strip_rows, col_step : col_step + COLS]
    filtered = total / 9.0
    return remove_background(
        lax.all_to_all(filtered, "sub", split_axis=2, concat_axis=0, tiled=True)
    )


def solution(mesh):
    in_specs = (P("sub", "strip", None), P("sub"))
    out_specs = P("strip", "sub", None)
    return jax.shard_map(body, mesh=mesh, in_specs=in_specs, out_specs=out_specs, check_vma=False)
```

profile of v0, /device:TPU:1, one launch (start us, length us, event | category | flops | bytes accessed | tf_op | source)
XLA Modules:
  0.0 272.1 jit_solution(287190779689159328)
XLA Ops:
  6.5 0.7 all-gather.2.cloned.1.call-update
  7.3 4.0 %fusion.15 = bf16[1024,256]{0,1:T(8,128)(2,1)S(1)} fusion(), kind=kLoop, calls=%fused_computation.27 | loop fusion | flops 4456448 | bytes 524288 | tf_op jit(solution)/shard_map/convert.9
  11.2 4.3 %negate_convert_fusion = (bf16[1024,256]{0,1:T(8,128)(2,1)S(1)}, bf16[1024,256]{0,1:T(8,128)(2,1)S(1)}) fusion(), kind=kLoop, calls=%fused_computation.21 | loop fusion | flops 5242880 | bytes 1048576 | tf_op jit(solution)/shard_map/convert.6
  15.6 0.8 fusion.55
  16.4 0.6 multiply_convert_fusion.2
  17.0 115.6 %all-gather.2.cloned.1.call-done = bf16[2,256,2048]{2,1,0:T(8,128)(2,1)} async-done(((bf16[2,32,2048]{2,1,0:T(8,128)(2,1)}), bf16[2,256,2048]{2,1,0:T(8,128)(2,1)}) %all-gather.2.cloned.1.call-update) | async-done | bytes 2097168 | tf_op jit(solution)/shard_map/all_gather | solution.py:106
  132.6 2.9 %fusion.7 = f32[2,256,512]{1,2,0:T(8,128)S(1)} fusion(bf16[2,256,2048]{2,1,0:T(8,128)(2,1)} %all-gather.2.cloned.1.call-done, bf16[1024,256]{0,1:T(8,128)(2,1)S(1)} %get-tuple-element.16, bf16[1024,256]{0,1:T(8,128)(2,1)S(1)} %get-tuple-element.15, bf16[1024,256]{0,1:T(8,128)(2,1)S(1)} %fusion.15), kind=kOutput, calls=%fused_computation.11 | convolution fusion | flops 1082130432 | bytes 4718592 | tf_op jit(solution)/shard_map/skc,cn->skn/dot_general | solution.py:109
  135.6 0.3 convolution_bitcast_fusion
  136.1 4.1 %collective-permute-start = (f32[2,128,512]{1,2,0:T(8,128)S(1)}, f32[2,128,512]{1,2,0:T(8,128)S(1)}, u32[]{:S(2)}, u32[]{:S(2)}) collective-permute-start(f32[2,128,512]{1,2,0:T(8,128)S(1)} %pad_maximum_fusion), channel_id=1, source_target_pairs={{0,504},{8,0},{16,8},{24,16},{32,24},{40,32},{48,40},{56,48},{64,5... | collective-permute-start | bytes 1572872 | tf_op jit(solution)/shard_map/ppermute | solution.py:19
  140.2 6.4 %collective-permute-done = f32[2,128,512]{1,2,0:T(8,128)S(1)} collective-permute-done((f32[2,128,512]{1,2,0:T(8,128)S(1)}, f32[2,128,512]{1,2,0:T(8,128)S(1)}, u32[]{:S(2)}, u32[]{:S(2)}) %collective-permute-start) | collective-permute-done | bytes 524320 | tf_op jit(solution)/shard_map/ppermute | solution.py:19
  146.6 3.4 %collective-permute-start.1 = (f32[2,128,512]{1,2,0:T(8,128)S(1)}, f32[2,128,512]{1,2,0:T(8,128)S(1)}, u32[]{:S(2)}, u32[]{:S(2)}) collective-permute-start(f32[2,128,512]{1,2,0:T(8,128)S(1)} %collective-permute-done), channel_id=1, source_target_pairs={{0,504},{8,0},{16,8},{24,16},{32,24},{40,32},{48,40},{56,48},{64,5... | collective-permute-start | bytes 1572872 | tf_op jit(solution)/shard_map/ppermute | solution.py:19
  150.0 7.1 %collective-permute-done.1 = f32[2,128,512]{1,2,0:T(8,128)S(1)} collective-permute-done((f32[2,128,512]{1,2,0:T(8,128)S(1)}, f32[2,128,512]{1,2,0:T(8,128)S(1)}, u32[]{:S(2)}, u32[]{:S(2)}) %collective-permute-start.1) | collective-permute-done | bytes 524320 | tf_op jit(solution)/shard_map/ppermute | solution.py:19
  157.1 12.1 %collective-permute-start.2 = (f32[2,128,512]{1,2,0:T(8,128)S(1)}, f32[2,128,512]{1,2,0:T(8,128)S(1)}, u32[]{:S(2)}, u32[]{:S(2)}) collective-permute-start(f32[2,128,512]{1,2,0:T(8,128)S(1)} %collective-permute-done.1), channel_id=1, source_target_pairs={{0,504},{8,0},{16,8},{24,16},{32,24},{40,32},{48,40},{56,48},{64,5... | collective-permute-start | bytes 1572872 | tf_op jit(solution)/shard_map/ppermute | solution.py:19
  169.2 0.2 copy.34
  169.4 1.9 fusion.72
  171.3 0.2 copy.35
  171.6 2.0 convolution_add_fusion.3
  173.6 0.2 copy.36
  173.9 14.7 %collective-permute-start.3 = (f32[2,128,512]{1,2,0:T(8,128)S(1)}, f32[2,128,512]{1,2,0:T(8,128)S(1)}, u32[]{:S(2)}, u32[]{:S(2)}) collective-permute-start(f32[2,128,512]{1,2,0:T(8,128)S(1)} %collective-permute-done.2), channel_id=1, source_target_pairs={{0,504},{8,0},{16,8},{24,16},{32,24},{40,32},{48,40},{56,48},{64,5... | collective-permute-start | bytes 1572872 | tf_op jit(solution)/shard_map/ppermute | solution.py:19
  188.6 2.0 convolution_add_fusion.2
  190.6 0.2 copy.37
  190.8 2.0 convolution_add_fusion.1
  192.9 0.2 copy.38
  193.1 2.0 fusion.8
  195.4 8.6 %collective-permute-start.4 = (f32[2,1,256]{2,0,1:T(2,128)S(1)}, f32[2,1,256]{2,0,1:T(2,128)S(1)}, u32[]{:S(2)}, u32[]{:S(2)}) collective-permute-start(f32[2,1,256]{2,0,1:T(2,128)S(1)} %get-tuple-element.9), channel_id=1, source_target_pairs={{0,1},{1,2},{2,3},{3,4},{4,5},{5,6},{6,7},{8,9},{9,10},{10,11},{11... | collective-permute-start | bytes 6152 | tf_op jit(solution)/shard_map/ppermute | solution.py:29
  204.0 1.3 collective-permute-start.5
  205.3 11.7 %collective-permute-done.5 = f32[2,1,256]{2,0,1:T(2,128)S(1)} collective-permute-done((f32[2,1,256]{2,0,1:T(2,128)S(1)}, f32[2,1,256]{2,0,1:T(2,128)S(1)}, u32[]{:S(2)}, u32[]{:S(2)}) %collective-permute-start.5) | collective-permute-done | bytes 2080 | tf_op jit(solution)/shard_map/ppermute | solution.py:30
  217.0 0.5 select_maximum_fusion
  217.5 1.0 fusion.19
  218.6 45.0 %all_to_all.18 = f32[2,128,256]{1,0,2:T(2,128)S(1)} all-to-all(f32[2,128,256]{1,0,2:T(2,128)S(1)} %copy.39), channel_id=1, replica_groups=mesh['sub'=64,'strip'=8] {'sub'}, dimensions={2} | all-to-all | bytes 524288 | tf_op jit(solution)/shard_map/all_to_all | solution.py:138
  264.0 0.4 fusion.26
  264.4 0.9 copy.43
  (19 shorter events, 1.0 us)
Async XLA Ops:
  6.5 126.1 %all-gather.2.cloned.1.call-start = ((), (), s32[]{:S(2)}) async-start(), calls=%async_computation.1 | async-start | bytes 2359296 | tf_op jit(solution)/shard_map/all_gather | solution.py:106
  136.0 33.5 %copy-start = (f32[2,2,1]{1,0,2:T(2,128)S(1)}, f32[2,2,1]{1,0,2:T(2,128)}, u32[]{:S(2)}) copy-start(f32[2,2,1]{1,0,2:T(2,128)} %constant.88) | copy-start | bytes 52
  136.1 10.5 %collective-permute-start = (f32[2,128,512]{1,2,0:T(8,128)S(1)}, f32[2,128,512]{1,2,0:T(8,128)S(1)}, u32[]{:S(2)}, u32[]{:S(2)}) collective-permute-start(f32[2,128,512]{1,2,0:T(8,128)S(1)} %pad_maximum_fusion), channel_id=1, source_target_pairs={{0,504},{8,0},{16,8},{24,16},{32,24},{40,32},{48,40},{56,48},{64,5... | collective-permute-start | bytes 1572872 | tf_op jit(solution)/shard_map/ppermute | solution.py:19
  146.6 10.5 %collective-permute-start.1 = (f32[2,128,512]{1,2,0:T(8,128)S(1)}, f32[2,128,512]{1,2,0:T(8,128)S(1)}, u32[]{:S(2)}, u32[]{:S(2)}) collective-permute-start(f32[2,128,512]{1,2,0:T(8,128)S(1)} %collective-permute-done), channel_id=1, source_target_pairs={{0,504},{8,0},{16,8},{24,16},{32,24},{40,32},{48,40},{56,48},{64,5... | collective-permute-start | bytes 1572872 | tf_op jit(solution)/shard_map/ppermute | solution.py:19
  157.1 16.8 %collective-permute-start.2 = (f32[2,128,512]{1,2,0:T(8,128)S(1)}, f32[2,128,512]{1,2,0:T(8,128)S(1)}, u32[]{:S(2)}, u32[]{:S(2)}) collective-permute-start(f32[2,128,512]{1,2,0:T(8,128)S(1)} %collective-permute-done.1), channel_id=1, source_target_pairs={{0,504},{8,0},{16,8},{24,16},{32,24},{40,32},{48,40},{56,48},{64,5... | collective-permute-start | bytes 1572872 | tf_op jit(solution)/shard_map/ppermute | solution.py:19
  173.9 19.0 %collective-permute-start.3 = (f32[2,128,512]{1,2,0:T(8,128)S(1)}, f32[2,128,512]{1,2,0:T(8,128)S(1)}, u32[]{:S(2)}, u32[]{:S(2)}) collective-permute-start(f32[2,128,512]{1,2,0:T(8,128)S(1)} %collective-permute-done.2), channel_id=1, source_target_pairs={{0,504},{8,0},{16,8},{24,16},{32,24},{40,32},{48,40},{56,48},{64,5... | collective-permute-start | bytes 1572872 | tf_op jit(solution)/shard_map/ppermute | solution.py:19
  190.6 2.5 copy-start.1
  195.4 9.9 %collective-permute-start.4 = (f32[2,1,256]{2,0,1:T(2,128)S(1)}, f32[2,1,256]{2,0,1:T(2,128)S(1)}, u32[]{:S(2)}, u32[]{:S(2)}) collective-permute-start(f32[2,1,256]{2,0,1:T(2,128)S(1)} %get-tuple-element.9), channel_id=1, source_target_pairs={{0,1},{1,2},{2,3},{3,4},{4,5},{5,6},{6,7},{8,9},{9,10},{10,11},{11... | collective-permute-start | bytes 6152 | tf_op jit(solution)/shard_map/ppermute | solution.py:29
  204.0 13.0 %collective-permute-start.5 = (f32[2,1,256]{2,0,1:T(2,128)S(1)}, f32[2,1,256]{2,0,1:T(2,128)S(1)}, u32[]{:S(2)}, u32[]{:S(2)}) collective-permute-start(f32[2,1,256]{2,0,1:T(2,128)S(1)} %get-tuple-element.10), channel_id=1, source_target_pairs={{1,0},{2,1},{3,2},{4,3},{5,4},{6,5},{7,6},{9,8},{10,9},{11,10},{12... | collective-permute-start | bytes 6152 | tf_op jit(solution)/shard_map/ppermute | solution.py:30
Sparse Core Ops, SparseCore 0:
  10.6 121.9 all-gather.1
where the time goes:
time: 272 us
  waiting for transfers between devices  141 us (52%)
  blocking collectives  45 us (17%)
  starting transfers between devices  44.2 us (16%)
  between operations  13.7 us (5%)
  matrix products  13.6 us (5%)
  other arithmetic  11.6 us (4%)
    all_gather x1, waiting for transfers between devices, body(): piece = lax.all_gather(spectra, 'strip', axis=1, tiled=True)  116 us
    all_to_all x1, blocking collectives, body(): lax.all_to_all(filtered, 'sub', split_axis=2, concat_axis=0, tiled=True)  45 us
    ppermute x4, starting transfers between devices, from_behind(): return lax.ppermute(value, axis, pairs)  34.3 us
    ppermute x4, waiting for transfers between devices, from_behind(): return lax.ppermute(value, axis, pairs)  13.5 us
    ppermute x1, waiting for transfers between devices, extended(): after = lax.ppermute(leading, axis, down)  11.7 us
    another operation x4, other arithmetic  9.06 us
    ppermute x1, starting transfers between devices, extended(): before = lax.ppermute(last, axis, up)  8.55 us
    dot_general x4, matrix products, body(): jnp.einsum('ab,bmn->amn', jnp.asarray(window_mask(block_offset, sub_dev))...  8.05 us
  transfers between devices with their start and end apart: 7, of which 4 were waited for; matrix products, arithmetic and copies ran while one was open for 7% of the time, Pallas kernels for 0%

commit v1 on v0

v1 whole, which is shorter than its diff:
```python
import math

import jax
import jax.numpy as jnp
import numpy as np
import ml_dtypes
from jax import lax
from jax.experimental import pallas as pl
from jax.experimental.pallas import tpu as pltpu
from jax.sharding import Mesh, PartitionSpec as P

KR = 256
KA = 1024
ROWS = 1024
COLS = 256
WIN = 8
BG = 16
SUBAP = 128
SUBS = 64
STRIPS = 8
OWN_S = SUBAP // SUBS
OWN_K = KR // STRIPS
OWN_C = COLS // SUBS
OWN_R = ROWS // STRIPS
EXT_C = OWN_C + 2
EXT_R = OWN_R + 8
LANES = 128
HALF = 64


def column_matrix():
    n = np.arange(KA)[None, :]
    col = (np.arange(SUBS)[None, :] * OWN_C + np.arange(OWN_C)[:, None]).reshape(-1, 1)
    phase = ((n * col) % KA).astype(np.float64) * (2.0 * math.pi / KA)
    scale = 1.0 / math.sqrt(KA)
    return np.concatenate([np.cos(phase) * scale, -np.sin(phase) * scale], axis=1).astype(ml_dtypes.bfloat16)


def row_matrices():
    scale = 1.0 / math.sqrt(KR)
    k = np.arange(KR)[None, :] - KR // 2
    out = np.zeros((STRIPS, 2, EXT_R, STRIPS, 2, OWN_K), np.float64)
    for strip in range(STRIPS):
        m = strip * OWN_R - 1 + np.arange(OWN_R + 2)
        valid = ((m >= 0) & (m < ROWS)).astype(np.float64)[:, None]
        phase = ((m[:, None] * k) % ROWS).astype(np.float64) * (2.0 * math.pi / ROWS)
        cosine = (np.cos(phase) * scale * valid).reshape(-1, STRIPS, OWN_K)
        sine = (np.sin(phase) * scale * valid).reshape(-1, STRIPS, OWN_K)
        n = OWN_R + 2
        out[strip, 0, :n, :, 0] = cosine
        out[strip, 0, :n, :, 1] = -sine
        out[strip, 1, :n, :, 0] = sine
        out[strip, 1, :n, :, 1] = cosine
    return out.reshape(STRIPS, 2 * EXT_R, 2 * KR).astype(ml_dtypes.bfloat16)


def window_matrix():
    frame = np.arange(SUBAP)[:, None]
    sub = (np.arange(SUBS)[None, :] * OWN_S + np.arange(OWN_S)[:, None]).reshape(1, -1)
    return (((sub - frame) % SUBAP) < WIN).astype(ml_dtypes.bfloat16)


def columns_kernel(strip_ref, offsets_ref, spectra_ref, table_ref, out_ref):
    parts = []
    for swapped in (False, True):
        for s in range(OWN_S):
            re = spectra_ref[s, :, :KA]
            im = spectra_ref[s, :, KA:]
            upper = jnp.concatenate([re, -im], axis=1)
            if swapped:
                parts += [jnp.concatenate([-im, -re], axis=1), upper]
            else:
                parts += [upper, jnp.concatenate([im, re], axis=1)]
    stack = jnp.concatenate(parts, axis=0)
    mixed = lax.dot_general(table_ref[...], stack, (((1,), (1,)), ((), ())), preferred_element_type=jnp.float32)
    lane = lax.broadcasted_iota(jnp.int32, (8, LANES), 1)
    sample = (lane & (OWN_K - 1)) + strip_ref[0] * OWN_K - KR // 2
    offset = jnp.where(lane < HALF, offsets_ref[0], offsets_ref[1])
    angle = ((offset * sample) & (ROWS - 1)).astype(jnp.float32) * (2.0 * math.pi / ROWS)
    cosine = jnp.cos(angle)[:1]
    sine = jnp.sin(angle)[:1]
    own = []
    for c in range(OWN_C):
        block = mixed[c * SUBS : (c + 1) * SUBS]
        own.append(block[:, :LANES] * cosine + block[:, LANES:] * sine)
    zero = jnp.zeros((1, LANES), jnp.float32)
    before = jnp.concatenate([zero, own[-1][: SUBS - 1]], axis=0)
    after = jnp.concatenate([own[0][1:], zero], axis=0)
    ext = [before] + own + [after]
    first = lax.broadcasted_iota(jnp.int32, (SUBS, LANES), 1) < HALF
    for j in range(EXT_C // 2):
        a, b = ext[2 * j], ext[2 * j + 1]
        for p, slab in ((0, jnp.where(first, a, pltpu.roll(b, HALF, 1))), (1, jnp.where(first, pltpu.roll(a, HALF, 1), b))):
            slab = slab.astype(jnp.bfloat16)
            at = (p * (EXT_C // 2) + j) * LANES
            for half in range(2):
                out_ref[half * SUBS : (half + 1) * SUBS, at : at + LANES] = slab


def image_kernel(data_ref, table_ref, window_ref, out_ref):
    pairs = EXT_C // 2
    width = pairs * LANES
    window = window_ref[...]
    summed = []
    for st in range(STRIPS):
        block = data_ref[st * SUBS : (st + 1) * SUBS, :]
        both = jnp.concatenate([block[:, :width], block[:, width:]], axis=0)
        summed.append(jnp.dot(window, both, preferred_element_type=jnp.float32))
    first = lax.broadcasted_iota(jnp.int32, (SUBAP, LANES), 1) < HALF
    logs = []
    for c in range(EXT_C):
        at = (c // 2) * LANES
        lanes = []
        for st in range(0, STRIPS, 2):
            a = summed[st][:, at : at + LANES]
            b = summed[st + 1][:, at : at + LANES]
            if c % 2 == 0:
                both = jnp.where(first, a, pltpu.roll(b, HALF, 1))
            else:
                both = jnp.where(first, pltpu.roll(a, HALF, 1), b)
            lanes.append(both.astype(jnp.bfloat16))
        frames = lax.dot_general(
            table_ref[...],
            jnp.concatenate(lanes, axis=1),
            (((1,), (1,)), ((), ())),
            preferred_element_type=jnp.float32,
        )
        re, im = frames[:EXT_R], frames[EXT_R:]
        logs.append(jnp.log(1.0 + re * re + im * im))
    for c in range(OWN_C):
        column = logs[c] + logs[c + 1] + logs[c + 2]
        total = column[:OWN_R] + column[1 : OWN_R + 1] + column[2 : OWN_R + 2]
        filtered = total * (1.0 / 9.0)
        back = filtered
        for step in (1, 2, 4, 8):
            back = back + pltpu.roll(back, step, 1)
        out_ref[:, c, :] = filtered - back * (1.0 / BG)


def body(spectra, offsets):
    strip = lax.axis_index("x") * 2 + lax.axis_index("zh")
    rows = lax.dynamic_index_in_dim(jnp.asarray(row_matrices()), strip, 0, keepdims=False)
    vmem = pl.BlockSpec(memory_space=pltpu.VMEM)
    smem = pl.BlockSpec(memory_space=pltpu.SMEM)
    sent = pl.pallas_call(
        columns_kernel,
        out_shape=jax.ShapeDtypeStruct((2 * SUBS, EXT_C * LANES), jnp.bfloat16),
        in_specs=[smem, smem, vmem, vmem],
        out_specs=vmem,
    )(strip.reshape(1), offsets, spectra, jnp.asarray(column_matrix()))
    sent = sent.reshape(2 * SUBS, 2, EXT_C * HALF)
    got = lax.all_to_all(sent, ("zh", "sub"), 0, 0, tiled=True)
    got = got.reshape(2 * SUBS, EXT_C * LANES)
    data = lax.all_gather(got, "x", axis=0, tiled=True)
    return pl.pallas_call(
        image_kernel,
        out_shape=jax.ShapeDtypeStruct((OWN_R, OWN_C, SUBAP), jnp.float32),
        in_specs=[vmem, vmem, vmem],
        out_specs=vmem,
    )(data, rows, jnp.asarray(window_matrix()))


def solution(mesh):
    grid = Mesh(mesh.devices.reshape(SUBS, STRIPS // 2, 2), ("sub", "x", "zh"))
    in_specs = (P("sub", ("x", "zh"), None), P("sub"))
    out_specs = P(("x", "zh"), "sub", None)
    return jax.shard_map(body, mesh=grid, in_specs=in_specs, out_specs=out_specs, check_vma=False)
```

time: 272 us -> 61.9 us (0.23)
  the two profiles are of different devices: /device:TPU:1 before, /device:TPU:34 now
where the time goes in v1:
time: 61.9 us; the launch traced here: 61.6 us
  starting transfers between devices  19.2 us (31%)
  waiting for transfers between devices  18.1 us (29%)
  blocking collectives  15.1 us (24%)
  Pallas kernels  5.83 us (9%)
  local copies, waits for them, and re-layouts  3.35 us (5%)
    all_to_all x1, starting transfers between devices, body(): got = lax.all_to_all(sent, ('zh', 'sub'), 0, 0, tiled=True)  19.2 us
    all_to_all x1, waiting for transfers between devices, body(): got = lax.all_to_all(sent, ('zh', 'sub'), 0, 0, tiled=True)  18.1 us
    all_gather x1, blocking collectives, body(): data = lax.all_gather(got, 'x', axis=0, tiled=True)  15.1 us
    pallas_call x1, Pallas kernels, body(): pl.pallas_call(image_kernel, out_shape=jax.ShapeDtypeStruct((OWN_R, OWN_C...  3.27 us
    pallas_call x1, Pallas kernels, body(): pl.pallas_call(columns_kernel, out_shape=jax.ShapeDtypeStruct((2 * SUBS,...  2.55 us
    squeeze x1, local copies, waits for them, and re-layouts, body(): lax.dynamic_index_in_dim(jnp.asarray(row_matrices()), strip, 0, keepdims=...  1.68 us
    reshape x1, local copies, waits for them, and re-layouts, body(): sent = sent.reshape(2 * SUBS, 2, EXT_C * HALF)  1.64 us
  transfers between devices with their start and end apart: 1, of which 1 were waited for; matrix products, arithmetic and copies ran while one was open for 3% of the time, Pallas kernels for 0%

profile of v1, /device:TPU:34, one launch (start us, length us, event | category | flops | bytes accessed | tf_op | source)
XLA Modules:
  0.0 61.6 jit_solution(11260139509590249033)
XLA Ops:
  0.0 2.6 %shard_map.55 = bf16[128,768]{1,0:T(8,128)(2,1)} custom-call(s32[1]{0:T(128)} %bitcast.strip_ref, s32[2]{0:T(128)} %offsets_ref.1, bf16[2,32,2048]{2,1,0:T(8,128)(2,1)} %spectra_ref.1, bf16[256,2048]{1,0:T(8,128)(2,1)} %constant.23.clone.table_ref), custom_call_target="tpu_custom_call" | custom-call | tf_op jit(solution)/shard_map/pallas_call | solution.py:145
  2.6 1.6 %reshape.10 = bf16[128,2,384]{2,1,0:T(2,128)(2,1)} reshape(bf16[128,768]{1,0:T(8,128)(2,1)} %shard_map.55) | data formatting | bytes 393216 | tf_op jit(solution)/shard_map/reshape | solution.py:151
  4.2 19.2 %all-to-all-start = ((bf16[128,2,384]{2,1,0:T(2,128)(2,1)}), bf16[128,2,384]{2,1,0:T(2,128)(2,1)S(1)}, u32[]{:S(2)}, u32[]{:S(2)}) async-start(bf16[128,2,384]{2,1,0:T(2,128)(2,1)} %reshape.10), calls=%async_computation | async-start | bytes 393216 | tf_op jit(solution)/shard_map/all_to_all | solution.py:152
  23.4 1.7 %dynamic-slice_bitcast_fusion.table_ref = bf16[272,512]{1,0:T(8,128)(2,1)} fusion(bf16[8,272,512]{2,1,0:T(8,128)(2,1)} %constant.22.clone, s32[]{:T(128)S(6)} %select_n.4), kind=kLoop, calls=%fused_computation | loop fusion | bytes 557060 | tf_op jit(solution)/shard_map/jit(dynamic_index_in_dim)/squeeze | solution.py:142
  25.1 18.1 %all-to-all-done = bf16[128,2,384]{2,1,0:T(2,128)(2,1)S(1)} async-done(((bf16[128,2,384]{2,1,0:T(2,128)(2,1)}), bf16[128,2,384]{2,1,0:T(2,128)(2,1)S(1)}, u32[]{:S(2)}, u32[]{:S(2)}) %all-to-all-start) | async-done | bytes 196640 | tf_op jit(solution)/shard_map/all_to_all | solution.py:152
  43.2 15.1 %all_gather.3.data_ref = bf16[512,768]{1,0:T(8,128)(2,1)} all-gather(bf16[128,768]{1,0:T(8,128)(2,1)S(1)} %bitcast.6), channel_id=1, replica_groups=mesh['sub'=64,'x'=4,'zh'=2] {'x'}, dimensions={0}, use_global_device_ids=true | all-gather | bytes 983040 | tf_op jit(solution)/shard_map/all_gather | solution.py:154
  58.4 3.3 %shard_map.56 = f32[128,4,128]{2,1,0:T(4,128)} custom-call(bf16[512,768]{1,0:T(8,128)(2,1)} %all_gather.3.data_ref, bf16[272,512]{1,0:T(8,128)(2,1)} %dynamic-slice_bitcast_fusion.table_ref, bf16[128,128]{1,0:T(8,128)(2,1)} %constant.24.clone.window_ref), custom_call_target="tpu_custom_call" | custom-call | tf_op jit(solution)/shard_map/pallas_call | solution.py:155
  (1 shorter events, 0.0 us)
Async XLA Ops:
  4.2 39.0 %all-to-all-start = ((bf16[128,2,384]{2,1,0:T(2,128)(2,1)}), bf16[128,2,384]{2,1,0:T(2,128)(2,1)S(1)}, u32[]{:S(2)}, u32[]{:S(2)}) async-start(bf16[128,2,384]{2,1,0:T(2,128)(2,1)} %reshape.10), calls=%async_computation | async-start | bytes 393216 | tf_op jit(solution)/shard_map/all_to_all | solution.py:152

commit v2 on v1

--- a/solution.py
+++ b/solution.py
@@ -26,13 +26,22 @@
 EXT_R = OWN_R + 8
 LANES = 128
 HALF = 64
+ZL, YC, XS, ZH = 8, 8, 4, 2
+BLOCK = COLS // ZL
+PAIRS = BLOCK // 2 + 1
+PAD_PAIRS = 20
+CHUNK = OWN_S * PAD_PAIRS
+TILE = OWN_S * ZL
 
 
 def column_matrix():
     n = np.arange(KA)[None, :]
-    col = (np.arange(SUBS)[None, :] * OWN_C + np.arange(OWN_C)[:, None]).reshape(-1, 1)
+    pair = np.arange(PAD_PAIRS)[None, None, :]
+    slot = 2 * pair + np.arange(2)[:, None, None]
+    col = (np.arange(ZL)[None, :, None] * BLOCK - 1 + slot).reshape(-1, 1)
+    valid = np.broadcast_to(slot < BLOCK + 2, (2, ZL, PAD_PAIRS)).reshape(-1, 1) & (col >= 0) & (col < COLS)
     phase = ((n * col) % KA).astype(np.float64) * (2.0 * math.pi / KA)
-    scale = 1.0 / math.sqrt(KA)
+    scale = valid / math.sqrt(KA)
     return np.concatenate([np.cos(phase) * scale, -np.sin(phase) * scale], axis=1).astype(ml_dtypes.bfloat16)
 
 
@@ -56,8 +65,15 @@
 
 def window_matrix():
     frame = np.arange(SUBAP)[:, None]
-    sub = (np.arange(SUBS)[None, :] * OWN_S + np.arange(OWN_S)[:, None]).reshape(1, -1)
+    yc, p, z = np.meshgrid(np.arange(YC), np.arange(OWN_S), np.arange(ZL), indexing="ij")
+    sub = (OWN_S * (z * YC + yc) + p).reshape(1, -1)
     return (((sub - frame) % SUBAP) < WIN).astype(ml_dtypes.bfloat16)
+
+
+def order_matrix():
+    pair, p, z = np.meshgrid(np.arange(PAIRS), np.arange(OWN_S), np.arange(ZL), indexing="ij")
+    source = (z * OWN_S + p) * PAD_PAIRS + pair
+    return (source.reshape(-1, 1) == np.arange(ZL * CHUNK)[None, :]).astype(ml_dtypes.bfloat16)
 
 
 def columns_kernel(strip_ref, offsets_ref, spectra_ref, table_ref, out_ref):
@@ -79,33 +95,38 @@
     angle = ((offset * sample) & (ROWS - 1)).astype(jnp.float32) * (2.0 * math.pi / ROWS)
     cosine = jnp.cos(angle)[:1]
     sine = jnp.sin(angle)[:1]
-    own = []
-    for c in range(OWN_C):
-        block = mixed[c * SUBS : (c + 1) * SUBS]
-        own.append(block[:, :LANES] * cosine + block[:, LANES:] * sine)
-    zero = jnp.zeros((1, LANES), jnp.float32)
-    before = jnp.concatenate([zero, own[-1][: SUBS - 1]], axis=0)
-    after = jnp.concatenate([own[0][1:], zero], axis=0)
-    ext = [before] + own + [after]
-    first = lax.broadcasted_iota(jnp.int32, (SUBS, LANES), 1) < HALF
-    for j in range(EXT_C // 2):
-        a, b = ext[2 * j], ext[2 * j + 1]
-        for p, slab in ((0, jnp.where(first, a, pltpu.roll(b, HALF, 1))), (1, jnp.where(first, pltpu.roll(a, HALF, 1), b))):
-            slab = slab.astype(jnp.bfloat16)
-            at = (p * (EXT_C // 2) + j) * LANES
-            for half in range(2):
-                out_ref[half * SUBS : (half + 1) * SUBS, at : at + LANES] = slab
+    shifted = mixed[:, :LANES] * cosine + mixed[:, LANES:] * sine
+    rows = ZL * PAD_PAIRS
+    even, odd = shifted[:rows], shifted[rows:]
+    first = lax.broadcasted_iota(jnp.int32, (rows, LANES), 1) < HALF
+    slabs = (jnp.where(first, even, pltpu.roll(odd, HALF, 1)), jnp.where(first, pltpu.roll(even, HALF, 1), odd))
+    for z in range(ZL):
+        block = jnp.concatenate([slab[z * PAD_PAIRS : (z + 1) * PAD_PAIRS] for slab in slabs], axis=0).astype(jnp.bfloat16)
+        for half in range(ZH):
+            out_ref[half * ZL + z] = block
+
+
+def order_kernel(data_ref, order_ref, out_ref):
+    both = jnp.concatenate([data_ref[h * ZL : (h + 1) * ZL].reshape(ZL * CHUNK, LANES) for h in range(ZH)], axis=1)
+    rows = jnp.dot(order_ref[...], both, preferred_element_type=jnp.float32).astype(jnp.bfloat16)
+    for j in range(YC):
+        for t in range(EXT_C // 2):
+            for h in range(ZH):
+                tile = rows[(2 * j + t) * TILE : (2 * j + t + 1) * TILE, h * LANES : (h + 1) * LANES]
+                for x in range(XS):
+                    out_ref[x * YC + j, (t * ZH + h) * TILE : (t * ZH + h + 1) * TILE, :] = tile
 
 
 def image_kernel(data_ref, table_ref, window_ref, out_ref):
-    pairs = EXT_C // 2
-    width = pairs * LANES
     window = window_ref[...]
     summed = []
-    for st in range(STRIPS):
-        block = data_ref[st * SUBS : (st + 1) * SUBS, :]
-        both = jnp.concatenate([block[:, :width], block[:, width:]], axis=0)
-        summed.append(jnp.dot(window, both, preferred_element_type=jnp.float32))
+    for x in range(XS):
+        for h in range(ZH):
+            slabs = []
+            for t in range(EXT_C // 2):
+                at = (t * ZH + h) * TILE
+                slabs.append(jnp.concatenate([data_ref[x * YC + j, at : at + TILE, :] for j in range(YC)], axis=0))
+            summed.append(jnp.dot(window, jnp.concatenate(slabs, axis=1), preferred_element_type=jnp.float32))
     first = lax.broadcasted_iota(jnp.int32, (SUBAP, LANES), 1) < HALF
     logs = []
     for c in range(EXT_C):
@@ -138,20 +159,24 @@
 
 
 def body(spectra, offsets):
-    strip = lax.axis_index("x") * 2 + lax.axis_index("zh")
+    strip = lax.axis_index("x") * ZH + lax.axis_index("zh")
     rows = lax.dynamic_index_in_dim(jnp.asarray(row_matrices()), strip, 0, keepdims=False)
     vmem = pl.BlockSpec(memory_space=pltpu.VMEM)
     smem = pl.BlockSpec(memory_space=pltpu.SMEM)
     sent = pl.pallas_call(
         columns_kernel,
-        out_shape=jax.ShapeDtypeStruct((2 * SUBS, EXT_C * LANES), jnp.bfloat16),
+        out_shape=jax.ShapeDtypeStruct((ZH * ZL, CHUNK, LANES), jnp.bfloat16),
         in_specs=[smem, smem, vmem, vmem],
         out_specs=vmem,
     )(strip.reshape(1), offsets, spectra, jnp.asarray(column_matrix()))
-    sent = sent.reshape(2 * SUBS, 2, EXT_C * HALF)
-    got = lax.all_to_all(sent, ("zh", "sub"), 0, 0, tiled=True)
-    got = got.reshape(2 * SUBS, EXT_C * LANES)
-    data = lax.all_gather(got, "x", axis=0, tiled=True)
+    got = lax.all_to_all(sent, ("zh", "zl"), 0, 0, tiled=True)
+    sent = pl.pallas_call(
+        order_kernel,
+        out_shape=jax.ShapeDtypeStruct((XS * YC, EXT_C // 2 * ZH * TILE, LANES), jnp.bfloat16),
+        in_specs=[vmem, vmem],
+        out_specs=vmem,
+    )(got, jnp.asarray(order_matrix()))
+    data = lax.all_to_all(sent, ("x", "y", "co"), 0, 0, tiled=True)
     return pl.pallas_call(
         image_kernel,
         out_shape=jax.ShapeDtypeStruct((OWN_R, OWN_C, SUBAP), jnp.float32),
@@ -161,7 +186,7 @@
 
 
 def solution(mesh):
-    grid = Mesh(mesh.devices.reshape(SUBS, STRIPS // 2, 2), ("sub", "x", "zh"))
-    in_specs = (P("sub", ("x", "zh"), None), P("sub"))
-    out_specs = P(("x", "zh"), "sub", None)
+    grid = Mesh(mesh.devices.reshape(ZL, YC // 2, 2, XS, ZH), ("zl", "y", "co", "x", "zh"))
+    in_specs = (P(("zl", "y", "co"), ("x", "zh"), None), P(("zl", "y", "co")))
+    out_specs = P(("x", "zh"), ("zl", "y", "co"), None)
     return jax.shard_map(body, mesh=grid, in_specs=in_specs, out_specs=out_specs, check_vma=False)

time: 61.9 us -> 63.1 us (1.019)
  the two profiles are of different devices: /device:TPU:34 before, /device:TPU:1 now
where the time goes in v2:
time: 63.1 us; the launch traced here: 62.8 us
  blocking collectives  28.1 us (45%)
  waiting for transfers between devices  12.5 us (20%)
  starting transfers between devices  11.5 us (18%)
  Pallas kernels  8.11 us (13%)
  local copies, waits for them, and re-layouts  2.57 us (4%)
    all_to_all x1, blocking collectives, body(): got = lax.all_to_all(sent, ('zh', 'zl'), 0, 0, tiled=True)  28.1 us
    all_to_all x1, waiting for transfers between devices, body(): data = lax.all_to_all(sent, ('x', 'y', 'co'), 0, 0, tiled=True)  12.5 us
    all_to_all x1, starting transfers between devices, body(): data = lax.all_to_all(sent, ('x', 'y', 'co'), 0, 0, tiled=True)  11.5 us
    pallas_call x1, Pallas kernels, body(): pl.pallas_call(image_kernel, out_shape=jax.ShapeDtypeStruct((OWN_R, OWN_C...  3.27 us
    pallas_call x1, Pallas kernels, body(): pl.pallas_call(columns_kernel, out_shape=jax.ShapeDtypeStruct((ZH * ZL, C...  2.71 us
    pallas_call x1, Pallas kernels, body(): pl.pallas_call(order_kernel, out_shape=jax.ShapeDtypeStruct((XS * YC, EXT...  2.13 us
    squeeze x1, local copies, waits for them, and re-layouts, body(): lax.dynamic_index_in_dim(jnp.asarray(row_matrices()), strip, 0, keepdims=...  1.68 us
  transfers between devices with their start and end apart: 1, of which 1 were waited for; matrix products, arithmetic and copies ran while one was open for 3% of the time, Pallas kernels for 0%

profile of v2, /device:TPU:1, one launch (start us, length us, event | category | flops | bytes accessed | tf_op | source)
XLA Modules:
  0.0 62.8 jit_solution(11914462290409360231)
XLA Ops:
  0.0 2.7 %shard_map.64 = bf16[16,40,128]{2,1,0:T(8,128)(2,1)} custom-call(s32[1]{0:T(128)} %bitcast.strip_ref, s32[2]{0:T(128)} %offsets_ref.1, bf16[2,32,2048]{2,1,0:T(8,128)(2,1)} %spectra_ref.1, bf16[320,2048]{1,0:T(8,128)(2,1)} %constant.25.clone.table_ref), custom_call_target="tpu_custom_call" | custom-call | tf_op jit(solution)/shard_map/pallas_call | solution.py:166
  2.7 28.1 %all_to_all.10.data_ref = bf16[16,40,128]{2,1,0:T(8,128)(2,1)} all-to-all(bf16[16,40,128]{2,1,0:T(8,128)(2,1)} %shard_map.64), channel_id=1, replica_groups=mesh['zl'=8,'y'=4,'co'=2,'x'=4,'zh'=2] {'zh','zl'}, dimensions={0} | all-to-all | bytes 327680 | tf_op jit(solution)/shard_map/all_to_all | solution.py:172
  30.8 2.1 %shard_map.65 = bf16[32,96,128]{2,1,0:T(8,128)(2,1)} custom-call(bf16[16,40,128]{2,1,0:T(8,128)(2,1)} %all_to_all.10.data_ref, bf16[272,320]{1,0:T(8,128)(2,1)} %constant.26.clone.order_ref), custom_call_target="tpu_custom_call" | custom-call | tf_op jit(solution)/shard_map/pallas_call | solution.py:173
  32.9 11.5 %all-to-all-start.1 = ((bf16[32,96,128]{2,1,0:T(8,128)(2,1)}), bf16[32,96,128]{2,1,0:T(8,128)(2,1)S(1)}, u32[]{:S(2)}, u32[]{:S(2)}) async-start(bf16[32,96,128]{2,1,0:T(8,128)(2,1)} %shard_map.65), calls=%async_computation.1 | async-start | bytes 1572864 | tf_op jit(solution)/shard_map/all_to_all | solution.py:179
  44.4 1.7 %dynamic-slice_bitcast_fusion.table_ref = bf16[272,512]{1,0:T(8,128)(2,1)} fusion(bf16[8,272,512]{2,1,0:T(8,128)(2,1)} %constant.24.clone, s32[]{:T(128)S(6)} %select_n.4), kind=kLoop, calls=%fused_computation | loop fusion | bytes 557060 | tf_op jit(solution)/shard_map/jit(dynamic_index_in_dim)/squeeze | solution.py:163
  46.1 12.5 %all-to-all-done.1.data_ref = bf16[32,96,128]{2,1,0:T(8,128)(2,1)S(1)} async-done(((bf16[32,96,128]{2,1,0:T(8,128)(2,1)}), bf16[32,96,128]{2,1,0:T(8,128)(2,1)S(1)}, u32[]{:S(2)}, u32[]{:S(2)}) %all-to-all-start.1) | async-done | bytes 786464 | tf_op jit(solution)/shard_map/all_to_all | solution.py:179
  58.6 0.0 copy-start
  58.6 0.9 %copy-done = bf16[32,96,128]{2,1,0:T(8,128)(2,1)} copy-done((bf16[32,96,128]{2,1,0:T(8,128)(2,1)}, bf16[32,96,128]{2,1,0:T(8,128)(2,1)S(1)}, u32[]{:S(2)}) %copy-start) | copy-done | bytes 786456
  59.5 3.3 %shard_map.66 = f32[128,4,128]{2,1,0:T(4,128)} custom-call(bf16[32,96,128]{2,1,0:T(8,128)(2,1)} %copy-done, bf16[272,512]{1,0:T(8,128)(2,1)} %dynamic-slice_bitcast_fusion.table_ref, bf16[128,128]{1,0:T(8,128)(2,1)} %constant.27.clone.window_ref), custom_call_target="tpu_custom_call" | custom-call | tf_op jit(solution)/shard_map/pallas_call | solution.py:180
Async XLA Ops:
  32.9 25.7 %all-to-all-start.1 = ((bf16[32,96,128]{2,1,0:T(8,128)(2,1)}), bf16[32,96,128]{2,1,0:T(8,128)(2,1)S(1)}, u32[]{:S(2)}, u32[]{:S(2)}) async-start(bf16[32,96,128]{2,1,0:T(8,128)(2,1)} %shard_map.65), calls=%async_computation.1 | async-start | bytes 1572864 | tf_op jit(solution)/shard_map/all_to_all | solution.py:179
  58.6 0.9 %copy-start = (bf16[32,96,128]{2,1,0:T(8,128)(2,1)}, bf16[32,96,128]{2,1,0:T(8,128)(2,1)S(1)}, u32[]{:S(2)}) copy-start(bf16[32,96,128]{2,1,0:T(8,128)(2,1)S(1)} %all-to-all-done.1.data_ref) | copy-start | bytes 2359300

commit v3 on v2

--- a/solution.py
+++ b/solution.py
@@ -24,6 +24,7 @@
 OWN_R = ROWS // STRIPS
 EXT_C = OWN_C + 2
 EXT_R = OWN_R + 8
+VMEM_BYTES = 24 << 20
 LANES = 128
 HALF = 64
 ZL, YC, XS, ZH = 8, 8, 4, 2
@@ -64,19 +65,36 @@
 
 
 def window_matrix():
-    frame = np.arange(SUBAP)[:, None]
-    yc, p, z = np.meshgrid(np.arange(YC), np.arange(OWN_S), np.arange(ZL), indexing="ij")
-    sub = (OWN_S * (z * YC + yc) + p).reshape(1, -1)
-    return (((sub - frame) % SUBAP) < WIN).astype(ml_dtypes.bfloat16)
+    frame = lax.broadcasted_iota(jnp.int32, (SUBAP, SUBAP), 0)
+    lane = lax.broadcasted_iota(jnp.int32, (SUBAP, SUBAP), 1)
+    sub = OWN_S * ((lane & (ZL - 1)) * YC + (lane >> 4)) + ((lane >> 3) & 1)
+    return jnp.where(((sub - frame) & (SUBAP - 1)) < WIN, 1.0, 0.0).astype(jnp.bfloat16)
 
 
 def order_matrix():
-    pair, p, z = np.meshgrid(np.arange(PAIRS), np.arange(OWN_S), np.arange(ZL), indexing="ij")
-    source = (z * OWN_S + p) * PAD_PAIRS + pair
-    return (source.reshape(-1, 1) == np.arange(ZL * CHUNK)[None, :]).astype(ml_dtypes.bfloat16)
-
-
-def columns_kernel(strip_ref, offsets_ref, spectra_ref, table_ref, out_ref):
+    row = lax.broadcasted_iota(jnp.int32, (PAIRS * TILE, ZL * CHUNK), 0)
+    lane = lax.broadcasted_iota(jnp.int32, (PAIRS * TILE, ZL * CHUNK), 1)
+    source = ((row & (ZL - 1)) * OWN_S + ((row >> 3) & 1)) * PAD_PAIRS + (row >> 4)
+    return jnp.where(source == lane, 1.0, 0.0).astype(jnp.bfloat16)
+
+
+def columns_kernel(strip_ref, offsets_hbm, spectra_hbm, table_hbm, out_ref, offsets_ref, spectra_ref, table_ref, arrived):
+    rows = ZL * PAD_PAIRS
+    fetches = [pltpu.make_async_copy(spectra_hbm, spectra_ref, arrived.at[0])]
+    for i in range(2):
+        part = pl.ds(i * rows, rows)
+        fetches.append(pltpu.make_async_copy(table_hbm.at[part], table_ref.at[part], arrived.at[i + 1]))
+    small = pltpu.make_async_copy(offsets_hbm, offsets_ref, arrived.at[3])
+    for fetch in [small] + fetches:
+        fetch.start()
+    small.wait()
+    lane = lax.broadcasted_iota(jnp.int32, (8, LANES), 1)
+    sample = (lane & (OWN_K - 1)) + strip_ref[0] * OWN_K - KR // 2
+    offset = jnp.where(lane < HALF, offsets_ref[0], offsets_ref[1])
+    angle = ((offset * sample) & (ROWS - 1)).astype(jnp.float32) * (2.0 * math.pi / ROWS)
+    cosine = jnp.cos(angle)[:1]
+    sine = jnp.sin(angle)[:1]
+    fetches[0].wait()
     parts = []
     for swapped in (False, True):
         for s in range(OWN_S):
@@ -88,16 +106,14 @@
             else:
                 parts += [upper, jnp.concatenate([im, re], axis=1)]
     stack = jnp.concatenate(parts, axis=0)
-    mixed = lax.dot_general(table_ref[...], stack, (((1,), (1,)), ((), ())), preferred_element_type=jnp.float32)
-    lane = lax.broadcasted_iota(jnp.int32, (8, LANES), 1)
-    sample = (lane & (OWN_K - 1)) + strip_ref[0] * OWN_K - KR // 2
-    offset = jnp.where(lane < HALF, offsets_ref[0], offsets_ref[1])
-    angle = ((offset * sample) & (ROWS - 1)).astype(jnp.float32) * (2.0 * math.pi / ROWS)
-    cosine = jnp.cos(angle)[:1]
-    sine = jnp.sin(angle)[:1]
-    shifted = mixed[:, :LANES] * cosine + mixed[:, LANES:] * sine
-    rows = ZL * PAD_PAIRS
-    even, odd = shifted[:rows], shifted[rows:]
+    shifted = []
+    for i in range(2):
+        fetches[i + 1].wait()
+        mixed = lax.dot_general(
+            table_ref[i * rows : (i + 1) * rows], stack, (((1,), (1,)), ((), ())), preferred_element_type=jnp.float32
+        )
+        shifted.append(mixed[:, :LANES] * cosine + mixed[:, LANES:] * sine)
+    even, odd = shifted
     first = lax.broadcasted_iota(jnp.int32, (rows, LANES), 1) < HALF
     slabs = (jnp.where(first, even, pltpu.roll(odd, HALF, 1)), jnp.where(first, pltpu.roll(even, HALF, 1), odd))
     for z in range(ZL):
@@ -106,9 +122,9 @@
             out_ref[half * ZL + z] = block
 
 
-def order_kernel(data_ref, order_ref, out_ref):
+def order_kernel(data_ref, out_ref):
     both = jnp.concatenate([data_ref[h * ZL : (h + 1) * ZL].reshape(ZL * CHUNK, LANES) for h in range(ZH)], axis=1)
-    rows = jnp.dot(order_ref[...], both, preferred_element_type=jnp.float32).astype(jnp.bfloat16)
+    rows = jnp.dot(order_matrix(), both, preferred_element_type=jnp.float32).astype(jnp.bfloat16)
     for j in range(YC):
         for t in range(EXT_C // 2):
             for h in range(ZH):
@@ -117,8 +133,10 @@
                     out_ref[x * YC + j, (t * ZH + h) * TILE : (t * ZH + h + 1) * TILE, :] = tile
 
 
-def image_kernel(data_ref, table_ref, window_ref, out_ref):
-    window = window_ref[...]
+def image_kernel(strip_ref, data_ref, tables_ref, out_ref, table_ref, arrived):
+    fetch = pltpu.make_async_copy(tables_ref.at[strip_ref[0]], table_ref, arrived)
+    fetch.start()
+    window = window_matrix()
     summed = []
     for x in range(XS):
         for h in range(ZH):
@@ -128,6 +146,7 @@
                 slabs.append(jnp.concatenate([data_ref[x * YC + j, at : at + TILE, :] for j in range(YC)], axis=0))
             summed.append(jnp.dot(window, jnp.concatenate(slabs, axis=1), preferred_element_type=jnp.float32))
     first = lax.broadcasted_iota(jnp.int32, (SUBAP, LANES), 1) < HALF
+    fetch.wait()
     logs = []
     for c in range(EXT_C):
         at = (c // 2) * LANES
@@ -159,30 +178,47 @@
 
 
 def body(spectra, offsets):
-    strip = lax.axis_index("x") * ZH + lax.axis_index("zh")
-    rows = lax.dynamic_index_in_dim(jnp.asarray(row_matrices()), strip, 0, keepdims=False)
+    strip = (lax.axis_index("x") * ZH + lax.axis_index("zh")).reshape(1)
     vmem = pl.BlockSpec(memory_space=pltpu.VMEM)
     smem = pl.BlockSpec(memory_space=pltpu.SMEM)
+    hbm = pl.BlockSpec(memory_space=pltpu.HBM)
+    params = pltpu.CompilerParams(vmem_limit_bytes=VMEM_BYTES)
+    columns = jnp.asarray(column_matrix())
     sent = pl.pallas_call(
         columns_kernel,
         out_shape=jax.ShapeDtypeStruct((ZH * ZL, CHUNK, LANES), jnp.bfloat16),
-        in_specs=[smem, smem, vmem, vmem],
+        in_specs=[smem, hbm, hbm, hbm],
         out_specs=vmem,
-    )(strip.reshape(1), offsets, spectra, jnp.asarray(column_matrix()))
+        scratch_shapes=[
+            pltpu.SMEM(offsets.shape, jnp.int32),
+            pltpu.VMEM(spectra.shape, jnp.bfloat16),
+            pltpu.VMEM(columns.shape, jnp.bfloat16),
+            pltpu.SemaphoreType.DMA((4,)),
+        ],
+        compiler_params=params,
+    )(
+        strip,
+        pltpu.with_memory_space_constraint(offsets, pltpu.HBM),
+        pltpu.with_memory_space_constraint(spectra, pltpu.HBM),
+        pltpu.with_memory_space_constraint(columns, pltpu.HBM),
+    )
     got = lax.all_to_all(sent, ("zh", "zl"), 0, 0, tiled=True)
     sent = pl.pallas_call(
         order_kernel,
         out_shape=jax.ShapeDtypeStruct((XS * YC, EXT_C // 2 * ZH * TILE, LANES), jnp.bfloat16),
-        in_specs=[vmem, vmem],
+        in_specs=[vmem],
         out_specs=vmem,
-    )(got, jnp.asarray(order_matrix()))
+        compiler_params=params,
+    )(got)
     data = lax.all_to_all(sent, ("x", "y", "co"), 0, 0, tiled=True)
     return pl.pallas_call(
         image_kernel,
         out_shape=jax.ShapeDtypeStruct((OWN_R, OWN_C, SUBAP), jnp.float32),
-        in_specs=[vmem, vmem, vmem],
+        in_specs=[smem, vmem, hbm],
         out_specs=vmem,
-    )(data, rows, jnp.asarray(window_matrix()))
+        scratch_shapes=[pltpu.VMEM((2 * EXT_R, 2 * KR), jnp.bfloat16), pltpu.SemaphoreType.DMA],
+        compiler_params=params,
+    )(strip, data, pltpu.with_memory_space_constraint(jnp.asarray(row_matrices()), pltpu.HBM))
 
 
 def solution(mesh):

time: 63.1 us -> 59.3 us (0.940)
  blocking collectives: 28.1 us -> 53.2 us
  waiting for transfers between devices: 12.5 us -> 0 us
  starting transfers between devices: 11.5 us -> 0 us
  local copies, waits for them, and re-layouts: 2.57 us -> 0 us
  Pallas kernels: 8.11 us -> 5.82 us
    all_to_all x0 -> x1, blocking collectives: none -> 25.5 us  [body(): data = lax.all_to_all(sent, ('x', 'y', 'co'), 0, 0, tiled=True)]
    all_to_all x1 -> x0, waiting for transfers between devices: 12.5 us -> none  [body(): data = lax.all_to_all(sent, ('x', 'y', 'co'), 0, 0, tiled=True)]
    all_to_all x1 -> x0, starting transfers between devices: 11.5 us -> none  [body(): data = lax.all_to_all(sent, ('x', 'y', 'co'), 0, 0, tiled=True)]
    pallas_call x1, Pallas kernels: 2.13 us -> 0.22 us  [body(): pl.pallas_call(order_kernel, out_shape=jax.ShapeDtypeStruct((XS * YC, EXT...]
    squeeze x1 -> x0, local copies, waits for them, and re-layouts: 1.68 us -> none  [body(): lax.dynamic_index_in_dim(jnp.asarray(row_matrices()), strip, 0, keepdims=...]
    unnamed x2 -> x0, local copies, waits for them, and re-layouts: 0.89 us -> none
  transfers between devices with their start and end apart: 1 -> 0, of which waited for: 1 -> 0; matrix products, arithmetic and copies ran while one was open for 3% -> 0% of each run, Pallas kernels for 0% -> 0%
where the time goes in v3:
time: 59.3 us; the launch traced here: 59.1 us
  blocking collectives  53.2 us (90%)
  Pallas kernels  5.82 us (10%)
    all_to_all x1, blocking collectives, body(): got = lax.all_to_all(sent, ('zh', 'zl'), 0, 0, tiled=True)  27.8 us
    all_to_all x1, blocking collectives, body(): data = lax.all_to_all(sent, ('x', 'y', 'co'), 0, 0, tiled=True)  25.5 us
    pallas_call x1, Pallas kernels, body(): pl.pallas_call(image_kernel, out_shape=jax.ShapeDtypeStruct((OWN_R, OWN_C...  2.89 us
    pallas_call x1, Pallas kernels, body(): pl.pallas_call(columns_kernel, out_shape=jax.ShapeDtypeStruct((ZH * ZL, C...  2.71 us

profile of v3, /device:TPU:1, one launch (start us, length us, event | category | flops | bytes accessed | tf_op | source)
XLA Modules:
  0.0 59.1 jit_solution(12131354729687160336)
XLA Ops:
  0.0 2.7 %shard_map.46 = bf16[16,40,128]{2,1,0:T(8,128)(2,1)S(1)} custom-call(s32[1]{0:T(128)} %bitcast.strip_ref, s32[2]{0:T(128)} %offsets_hbm.1, bf16[2,32,2048]{2,1,0:T(8,128)(2,1)} %spectra_hbm.1, bf16[320,2048]{1,0:T(8,128)(2,1)} %constant.14.clone.table_hbm), custom_call_target="tpu_custom_call" | custom-call | tf_op jit(solution)/shard_map/pallas_call | solution.py:187
  2.7 27.8 %all_to_all.10.data_ref = bf16[16,40,128]{2,1,0:T(8,128)(2,1)S(1)} all-to-all(bf16[16,40,128]{2,1,0:T(8,128)(2,1)S(1)} %shard_map.46), channel_id=1, replica_groups=mesh['zl'=8,'y'=4,'co'=2,'x'=4,'zh'=2] {'zh','zl'}, dimensions={0} | all-to-all | bytes 327680 | tf_op jit(solution)/shard_map/all_to_all | solution.py:205
  30.5 0.2 shard_map.47
  30.7 25.5 %all_to_all.11.data_ref = bf16[32,96,128]{2,1,0:T(8,128)(2,1)S(1)} all-to-all(bf16[32,96,128]{2,1,0:T(8,128)(2,1)S(1)} %shard_map.47), channel_id=1, replica_groups=mesh['zl'=8,'y'=4,'co'=2,'x'=4,'zh'=2] {'x','y','co'}, dimensions={0} | all-to-all | bytes 1572864 | tf_op jit(solution)/shard_map/all_to_all | solution.py:213
  56.2 2.9 %shard_map.48 = f32[128,4,128]{2,1,0:T(4,128)} custom-call(s32[1]{0:T(128)} %bitcast.strip_ref, bf16[32,96,128]{2,1,0:T(8,128)(2,1)S(1)} %all_to_all.11.data_ref, bf16[8,272,512]{2,1,0:T(8,128)(2,1)} %constant.15.clone.tables_ref), custom_call_target="tpu_custom_call" | custom-call | tf_op jit(solution)/shard_map/pallas_call | solution.py:214

commit v4 on v3

--- a/solution.py
+++ b/solution.py
@@ -30,17 +30,15 @@
 ZL, YC, XS, ZH = 8, 8, 4, 2
 BLOCK = COLS // ZL
 PAIRS = BLOCK // 2 + 1
-PAD_PAIRS = 20
-CHUNK = OWN_S * PAD_PAIRS
+SLOTS = BLOCK + 4
 TILE = OWN_S * ZL
 
 
 def column_matrix():
     n = np.arange(KA)[None, :]
-    pair = np.arange(PAD_PAIRS)[None, None, :]
-    slot = 2 * pair + np.arange(2)[:, None, None]
-    col = (np.arange(ZL)[None, :, None] * BLOCK - 1 + slot).reshape(-1, 1)
-    valid = np.broadcast_to(slot < BLOCK + 2, (2, ZL, PAD_PAIRS)).reshape(-1, 1) & (col >= 0) & (col < COLS)
+    slot = np.arange(SLOTS)[None, :]
+    col = (np.arange(ZL)[:, None] * BLOCK - 1 + slot).reshape(-1, 1)
+    valid = np.broadcast_to(slot < BLOCK + 2, (ZL, SLOTS)).reshape(-1, 1) & (col >= 0) & (col < COLS)
     phase = ((n * col) % KA).astype(np.float64) * (2.0 * math.pi / KA)
     scale = valid / math.sqrt(KA)
     return np.concatenate([np.cos(phase) * scale, -np.sin(phase) * scale], axis=1).astype(ml_dtypes.bfloat16)
@@ -72,14 +70,14 @@
 
 
 def order_matrix():
-    row = lax.broadcasted_iota(jnp.int32, (PAIRS * TILE, ZL * CHUNK), 0)
-    lane = lax.broadcasted_iota(jnp.int32, (PAIRS * TILE, ZL * CHUNK), 1)
-    source = ((row & (ZL - 1)) * OWN_S + ((row >> 3) & 1)) * PAD_PAIRS + (row >> 4)
+    row = lax.broadcasted_iota(jnp.int32, (PAIRS * TILE, ZL * SLOTS), 0)
+    lane = lax.broadcasted_iota(jnp.int32, (PAIRS * TILE, ZL * SLOTS), 1)
+    source = (row & (ZL - 1)) * SLOTS + (row >> 3)
     return jnp.where(source == lane, 1.0, 0.0).astype(jnp.bfloat16)
 
 
 def columns_kernel(strip_ref, offsets_hbm, spectra_hbm, table_hbm, out_ref, offsets_ref, spectra_ref, table_ref, arrived):
-    rows = ZL * PAD_PAIRS
+    rows = ZL * SLOTS // 2
     fetches = [pltpu.make_async_copy(spectra_hbm, spectra_ref, arrived.at[0])]
     for i in range(2):
         part = pl.ds(i * rows, rows)
@@ -113,17 +111,19 @@
             table_ref[i * rows : (i + 1) * rows], stack, (((1,), (1,)), ((), ())), preferred_element_type=jnp.float32
         )
         shifted.append(mixed[:, :LANES] * cosine + mixed[:, LANES:] * sine)
-    even, odd = shifted
-    first = lax.broadcasted_iota(jnp.int32, (rows, LANES), 1) < HALF
-    slabs = (jnp.where(first, even, pltpu.roll(odd, HALF, 1)), jnp.where(first, pltpu.roll(even, HALF, 1), odd))
-    for z in range(ZL):
-        block = jnp.concatenate([slab[z * PAD_PAIRS : (z + 1) * PAD_PAIRS] for slab in slabs], axis=0).astype(jnp.bfloat16)
-        for half in range(ZH):
-            out_ref[half * ZL + z] = block
+    shifted = jnp.concatenate(shifted, axis=0)
+    turned = pltpu.roll(shifted, HALF, 1)
+    odd_row = lax.broadcasted_iota(jnp.int32, shifted.shape, 0) & 1
+    last = lax.broadcasted_iota(jnp.int32, shifted.shape, 1) >> 6
+    partner = jnp.where(odd_row == 1, pltpu.roll(turned, 1, 0), pltpu.roll(turned, 2 * rows - 1, 0))
+    result = jnp.where(odd_row == last, shifted, partner).astype(jnp.bfloat16).reshape(rows, 2, LANES)
+    for half in range(ZH):
+        out_ref[half * rows : (half + 1) * rows] = result
 
 
 def order_kernel(data_ref, out_ref):
-    both = jnp.concatenate([data_ref[h * ZL : (h + 1) * ZL].reshape(ZL * CHUNK, LANES) for h in range(ZH)], axis=1)
+    rows = ZL * SLOTS // 2
+    both = jnp.concatenate([data_ref[h * rows : (h + 1) * rows].reshape(2 * rows, LANES) for h in range(ZH)], axis=1)
     rows = jnp.dot(order_matrix(), both, preferred_element_type=jnp.float32).astype(jnp.bfloat16)
     for j in range(YC):
         for t in range(EXT_C // 2):
@@ -186,7 +186,7 @@
     columns = jnp.asarray(column_matrix())
     sent = pl.pallas_call(
         columns_kernel,
-        out_shape=jax.ShapeDtypeStruct((ZH * ZL, CHUNK, LANES), jnp.bfloat16),
+        out_shape=jax.ShapeDtypeStruct((ZH * ZL * SLOTS // 2, 2, LANES), jnp.bfloat16),
         in_specs=[smem, hbm, hbm, hbm],
         out_specs=vmem,
         scratch_shapes=[
@@ -202,14 +202,14 @@
         pltpu.with_memory_space_constraint(spectra, pltpu.HBM),
         pltpu.with_memory_space_constraint(columns, pltpu.HBM),
     )
-    got = lax.all_to_all(sent, ("zh", "zl"), 0, 0, tiled=True)
+    got = lax.all_to_all(sent.reshape(ZH * ZL, SLOTS // 2, 2, LANES), ("zh", "zl"), 0, 0, tiled=True)
     sent = pl.pallas_call(
         order_kernel,
         out_shape=jax.ShapeDtypeStruct((XS * YC, EXT_C // 2 * ZH * TILE, LANES), jnp.bfloat16),
         in_specs=[vmem],
         out_specs=vmem,
         compiler_params=params,
-    )(got)
+    )(got.reshape(sent.shape))
     data = lax.all_to_all(sent, ("x", "y", "co"), 0, 0, tiled=True)
     return pl.pallas_call(
         image_kernel,

time: 59.3 us -> 58.8 us (level)
  no operation moved by 1% of the time
where the time goes in v4:
time: 58.8 us; the launch traced here: 58.6 us
  blocking collectives  52.7 us (90%)
  Pallas kernels  5.86 us (10%)
    all_to_all x1, blocking collectives, body(): lax.all_to_all(sent.reshape(ZH * ZL, SLOTS // 2, 2, LANES), ('zh', 'zl'),...  27.6 us
    all_to_all x1, blocking collectives, body(): data = lax.all_to_all(sent, ('x', 'y', 'co'), 0, 0, tiled=True)  25.1 us
    pallas_call x1, Pallas kernels, body(): pl.pallas_call(image_kernel, out_shape=jax.ShapeDtypeStruct((OWN_R, OWN_C...  2.89 us
    pallas_call x1, Pallas kernels, body(): pl.pallas_call(columns_kernel, out_shape=jax.ShapeDtypeStruct((ZH * ZL *...  2.69 us

profile of v4, /device:TPU:1, one launch (start us, length us, event | category | flops | bytes accessed | tf_op | source)
XLA Modules:
  0.0 58.6 jit_solution(11160951541899766393)
XLA Ops:
  0.0 2.7 %shard_map.46 = bf16[288,2,128]{2,1,0:T(2,128)(2,1)S(1)} custom-call(s32[1]{0:T(128)} %bitcast.strip_ref, s32[2]{0:T(128)} %offsets_hbm.1, bf16[2,32,2048]{2,1,0:T(8,128)(2,1)} %spectra_hbm.1, bf16[288,2048]{1,0:T(8,128)(2,1)} %constant.14.clone.table_hbm), custom_call_target="tpu_custom_call" | custom-call | tf_op jit(solution)/shard_map/pallas_call | solution.py:187
  2.7 27.6 %all_to_all.10 = bf16[16,18,2,128]{3,2,1,0:T(2,128)(2,1)S(1)} all-to-all(bf16[16,18,2,128]{3,2,1,0:T(2,128)(2,1)S(1)} %bitcast.4), channel_id=1, replica_groups=mesh['zl'=8,'y'=4,'co'=2,'x'=4,'zh'=2] {'zh','zl'}, dimensions={0} | all-to-all | bytes 294912 | tf_op jit(solution)/shard_map/all_to_all | solution.py:205
  30.3 0.3 shard_map.47
  30.6 25.1 %all_to_all.11.data_ref = bf16[32,96,128]{2,1,0:T(8,128)(2,1)S(1)} all-to-all(bf16[32,96,128]{2,1,0:T(8,128)(2,1)S(1)} %shard_map.47), channel_id=1, replica_groups=mesh['zl'=8,'y'=4,'co'=2,'x'=4,'zh'=2] {'x','y','co'}, dimensions={0} | all-to-all | bytes 1572864 | tf_op jit(solution)/shard_map/all_to_all | solution.py:213
  55.7 2.9 %shard_map.48 = f32[128,4,128]{2,1,0:T(4,128)} custom-call(s32[1]{0:T(128)} %bitcast.strip_ref, bf16[32,96,128]{2,1,0:T(8,128)(2,1)S(1)} %all_to_all.11.data_ref, bf16[8,272,512]{2,1,0:T(8,128)(2,1)} %constant.15.clone.tables_ref), custom_call_target="tpu_custom_call" | custom-call | tf_op jit(solution)/shard_map/pallas_call | solution.py:214

commit v5 on v4

--- a/solution.py
+++ b/solution.py
@@ -41,7 +41,7 @@
     valid = np.broadcast_to(slot < BLOCK + 2, (ZL, SLOTS)).reshape(-1, 1) & (col >= 0) & (col < COLS)
     phase = ((n * col) % KA).astype(np.float64) * (2.0 * math.pi / KA)
     scale = valid / math.sqrt(KA)
-    return np.concatenate([np.cos(phase) * scale, -np.sin(phase) * scale], axis=1).astype(ml_dtypes.bfloat16)
+    return np.stack([np.cos(phase) * scale, -np.sin(phase) * scale]).astype(ml_dtypes.bfloat16)
 
 
 def row_matrices():
@@ -76,14 +76,14 @@
     return jnp.where(source == lane, 1.0, 0.0).astype(jnp.bfloat16)
 
 
-def columns_kernel(strip_ref, offsets_hbm, spectra_hbm, table_hbm, out_ref, offsets_ref, spectra_ref, table_ref, arrived):
-    rows = ZL * SLOTS // 2
-    fetches = [pltpu.make_async_copy(spectra_hbm, spectra_ref, arrived.at[0])]
-    for i in range(2):
-        part = pl.ds(i * rows, rows)
-        fetches.append(pltpu.make_async_copy(table_hbm.at[part], table_ref.at[part], arrived.at[i + 1]))
-    small = pltpu.make_async_copy(offsets_hbm, offsets_ref, arrived.at[3])
-    for fetch in [small] + fetches:
+def columns_kernel(
+    strip_ref, offsets_hbm, spectra_hbm, table_hbm, tables_hbm, out_ref, rows_ref, offsets_ref, spectra_ref, table_ref, arrived
+):
+    small = pltpu.make_async_copy(offsets_hbm, offsets_ref, arrived.at[0])
+    whole = pltpu.make_async_copy(spectra_hbm, spectra_ref, arrived.at[1])
+    rows = pltpu.make_async_copy(tables_hbm.at[strip_ref[0]], rows_ref, arrived.at[2])
+    fetches = [pltpu.make_async_copy(table_hbm.at[i], table_ref.at[i], arrived.at[3 + i]) for i in range(2)]
+    for fetch in [small, whole] + fetches + [rows]:
         fetch.start()
     small.wait()
     lane = lax.broadcasted_iota(jnp.int32, (8, LANES), 1)
@@ -91,34 +91,31 @@
     offset = jnp.where(lane < HALF, offsets_ref[0], offsets_ref[1])
     angle = ((offset * sample) & (ROWS - 1)).astype(jnp.float32) * (2.0 * math.pi / ROWS)
     cosine = jnp.cos(angle)[:1]
-    sine = jnp.sin(angle)[:1]
-    fetches[0].wait()
-    parts = []
-    for swapped in (False, True):
-        for s in range(OWN_S):
-            re = spectra_ref[s, :, :KA]
-            im = spectra_ref[s, :, KA:]
-            upper = jnp.concatenate([re, -im], axis=1)
-            if swapped:
-                parts += [jnp.concatenate([-im, -re], axis=1), upper]
-            else:
-                parts += [upper, jnp.concatenate([im, re], axis=1)]
-    stack = jnp.concatenate(parts, axis=0)
-    shifted = []
-    for i in range(2):
-        fetches[i + 1].wait()
-        mixed = lax.dot_general(
-            table_ref[i * rows : (i + 1) * rows], stack, (((1,), (1,)), ((), ())), preferred_element_type=jnp.float32
-        )
-        shifted.append(mixed[:, :LANES] * cosine + mixed[:, LANES:] * sine)
-    shifted = jnp.concatenate(shifted, axis=0)
+    sine = jnp.sin(angle)
+    sine = jnp.where((lane & OWN_K) == 0, -sine, sine)[:1]
+    whole.wait()
+    re = [spectra_ref[s, :, :KA] for s in range(OWN_S)]
+    im = [spectra_ref[s, :, KA:] for s in range(OWN_S)]
+    mixed = None
+    for fetch, part in zip(fetches, (0, 1)):
+        if part == 0:
+            stack = jnp.concatenate([re[0], im[0], re[1], im[1]], axis=0)
+        else:
+            stack = jnp.concatenate([-im[0], re[0], -im[1], re[1]], axis=0)
+        fetch.wait()
+        product = lax.dot_general(table_ref[part], stack, (((1,), (1,)), ((), ())), preferred_element_type=jnp.float32)
+        mixed = product if mixed is None else mixed + product
+    lanes = lax.broadcasted_iota(jnp.int32, mixed.shape, 1)
+    other = jnp.where((lanes & OWN_K) == 0, pltpu.roll(mixed, LANES - OWN_K, 1), pltpu.roll(mixed, OWN_K, 1))
+    shifted = mixed * cosine + other * sine
     turned = pltpu.roll(shifted, HALF, 1)
     odd_row = lax.broadcasted_iota(jnp.int32, shifted.shape, 0) & 1
-    last = lax.broadcasted_iota(jnp.int32, shifted.shape, 1) >> 6
-    partner = jnp.where(odd_row == 1, pltpu.roll(turned, 1, 0), pltpu.roll(turned, 2 * rows - 1, 0))
-    result = jnp.where(odd_row == last, shifted, partner).astype(jnp.bfloat16).reshape(rows, 2, LANES)
+    partner = jnp.where(odd_row == 1, pltpu.roll(turned, 1, 0), pltpu.roll(turned, ZL * SLOTS - 1, 0))
+    pairs = ZL * SLOTS // 2
+    result = jnp.where(odd_row == lanes >> 6, shifted, partner).astype(jnp.bfloat16).reshape(pairs, 2, LANES)
     for half in range(ZH):
-        out_ref[half * rows : (half + 1) * rows] = result
+        out_ref[half * pairs : (half + 1) * pairs] = result
+    rows.wait()
 
 
 def order_kernel(data_ref, out_ref):
@@ -133,9 +130,7 @@
                     out_ref[x * YC + j, (t * ZH + h) * TILE : (t * ZH + h + 1) * TILE, :] = tile
 
 
-def image_kernel(strip_ref, data_ref, tables_ref, out_ref, table_ref, arrived):
-    fetch = pltpu.make_async_copy(tables_ref.at[strip_ref[0]], table_ref, arrived)
-    fetch.start()
+def image_kernel(data_ref, table_ref, out_ref):
     window = window_matrix()
     summed = []
     for x in range(XS):
@@ -146,7 +141,6 @@
                 slabs.append(jnp.concatenate([data_ref[x * YC + j, at : at + TILE, :] for j in range(YC)], axis=0))
             summed.append(jnp.dot(window, jnp.concatenate(slabs, axis=1), preferred_element_type=jnp.float32))
     first = lax.broadcasted_iota(jnp.int32, (SUBAP, LANES), 1) < HALF
-    fetch.wait()
     logs = []
     for c in range(EXT_C):
         at = (c // 2) * LANES
@@ -184,24 +178,22 @@
     hbm = pl.BlockSpec(memory_space=pltpu.HBM)
     params = pltpu.CompilerParams(vmem_limit_bytes=VMEM_BYTES)
     columns = jnp.asarray(column_matrix())
-    sent = pl.pallas_call(
+    sent, rows = pl.pallas_call(
         columns_kernel,
-        out_shape=jax.ShapeDtypeStruct((ZH * ZL * SLOTS // 2, 2, LANES), jnp.bfloat16),
-        in_specs=[smem, hbm, hbm, hbm],
-        out_specs=vmem,
+        out_shape=[
+            jax.ShapeDtypeStruct((ZH * ZL * SLOTS // 2, 2, LANES), jnp.bfloat16),
+            jax.ShapeDtypeStruct((2 * EXT_R, 2 * KR), jnp.bfloat16),
+        ],
+        in_specs=[smem, hbm, hbm, hbm, hbm],
+        out_specs=[vmem, vmem],
         scratch_shapes=[
             pltpu.SMEM(offsets.shape, jnp.int32),
             pltpu.VMEM(spectra.shape, jnp.bfloat16),
             pltpu.VMEM(columns.shape, jnp.bfloat16),
-            pltpu.SemaphoreType.DMA((4,)),
+            pltpu.SemaphoreType.DMA((5,)),
         ],
         compiler_params=params,
-    )(
-        strip,
-        pltpu.with_memory_space_constraint(offsets, pltpu.HBM),
-        pltpu.with_memory_space_constraint(spectra, pltpu.HBM),
-        pltpu.with_memory_space_constraint(columns, pltpu.HBM),
-    )
+    )(strip, *(pltpu.with_memory_space_constraint(a, pltpu.HBM) for a in (offsets, spectra, columns, jnp.asarray(row_matrices()))))
     got = lax.all_to_all(sent.reshape(ZH * ZL, SLOTS // 2, 2, LANES), ("zh", "zl"), 0, 0, tiled=True)
     sent = pl.pallas_call(
         order_kernel,
@@ -214,11 +206,10 @@
     return pl.pallas_call(
         image_kernel,
         out_shape=jax.ShapeDtypeStruct((OWN_R, OWN_C, SUBAP), jnp.float32),
-        in_specs=[smem, vmem, hbm],
+        in_specs=[vmem, vmem],
         out_specs=vmem,
-        scratch_shapes=[pltpu.VMEM((2 * EXT_R, 2 * KR), jnp.bfloat16), pltpu.SemaphoreType.DMA],
         compiler_params=params,
-    )(strip, data, pltpu.with_memory_space_constraint(jnp.asarray(row_matrices()), pltpu.HBM))
+    )(data, rows)
 
 
 def solution(mesh):

time: 58.8 us -> 57.3 us (0.974)
  Pallas kernels: 5.86 us -> 4.34 us
    pallas_call x1, Pallas kernels: 2.89 us -> 2.05 us  [body(): pl.pallas_call(image_kernel, out_shape=jax.ShapeDtypeStruct((OWN_R, OWN_C...]
    pallas_call x1, Pallas kernels: 2.69 us -> 2.01 us  [body(): pl.pallas_call(columns_kernel, out_shape=[jax.ShapeDtypeStruct((ZH * ZL *...]
where the time goes in v5:
time: 57.3 us; the launch traced here: 57.1 us
  blocking collectives  52.7 us (92%)
  Pallas kernels  4.34 us (8%)
    all_to_all x1, blocking collectives, body(): lax.all_to_all(sent.reshape(ZH * ZL, SLOTS // 2, 2, LANES), ('zh', 'zl'),...  27.6 us
    all_to_all x1, blocking collectives, body(): data = lax.all_to_all(sent, ('x', 'y', 'co'), 0, 0, tiled=True)  25.1 us
    pallas_call x1, Pallas kernels, body(): pl.pallas_call(image_kernel, out_shape=jax.ShapeDtypeStruct((OWN_R, OWN_C...  2.05 us
    pallas_call x1, Pallas kernels, body(): pl.pallas_call(columns_kernel, out_shape=[jax.ShapeDtypeStruct((ZH * ZL *...  2.01 us

profile of v5, /device:TPU:1, one launch (start us, length us, event | category | flops | bytes accessed | tf_op | source)
XLA Modules:
  0.0 57.1 jit_solution(8487135024660831344)
XLA Ops:
  0.0 2.0 %shard_map.46 = (bf16[288,2,128]{2,1,0:T(2,128)(2,1)S(1)}, bf16[272,512]{1,0:T(8,128)(2,1)S(1)}) custom-call(s32[1]{0:T(128)} %bitcast.strip_ref, s32[2]{0:T(128)} %offsets_hbm.1, bf16[2,32,2048]{2,1,0:T(8,128)(2,1)} %spectra_hbm.1, bf16[2,288,1024]{2,1,0:T(8,128)(2,1)} %constant.14.clone.table_hbm, bf16[8,272,512]{2,1,0:T(8,128)(2,1)} %constant.15.clone.tables_hbm), custom_call_target="tpu_custom_call" | custom-call | tf_op jit(solution)/shard_map/pallas_call | solution.py:181
  2.0 27.6 %all_to_all.10 = bf16[16,18,2,128]{3,2,1,0:T(2,128)(2,1)S(1)} all-to-all(bf16[16,18,2,128]{3,2,1,0:T(2,128)(2,1)S(1)} %bitcast.4), channel_id=1, replica_groups=mesh['zl'=8,'y'=4,'co'=2,'x'=4,'zh'=2] {'zh','zl'}, dimensions={0} | all-to-all | bytes 294912 | tf_op jit(solution)/shard_map/all_to_all | solution.py:197
  29.7 0.3 shard_map.47
  30.0 25.1 %all_to_all.11.data_ref = bf16[32,96,128]{2,1,0:T(8,128)(2,1)S(1)} all-to-all(bf16[32,96,128]{2,1,0:T(8,128)(2,1)S(1)} %shard_map.47), channel_id=1, replica_groups=mesh['zl'=8,'y'=4,'co'=2,'x'=4,'zh'=2] {'x','y','co'}, dimensions={0} | all-to-all | bytes 1572864 | tf_op jit(solution)/shard_map/all_to_all | solution.py:205
  55.0 2.1 %shard_map.48 = f32[128,4,128]{2,1,0:T(4,128)} custom-call(bf16[32,96,128]{2,1,0:T(8,128)(2,1)S(1)} %all_to_all.11.data_ref, bf16[272,512]{1,0:T(8,128)(2,1)S(1)} %get-tuple-element.8.table_ref), custom_call_target="tpu_custom_call" | custom-call | tf_op jit(solution)/shard_map/pallas_call | solution.py:206

commit v6 on v5

--- a/solution.py
+++ b/solution.py
@@ -74,6 +74,34 @@
     lane = lax.broadcasted_iota(jnp.int32, (PAIRS * TILE, ZL * SLOTS), 1)
     source = (row & (ZL - 1)) * SLOTS + (row >> 3)
     return jnp.where(source == lane, 1.0, 0.0).astype(jnp.bfloat16)
+
+
+AXES = ("zl", "y", "co", "x", "zh")
+FIRST_Z = 8
+FIRST_X, FIRST_Y, FIRST_CO = 2, 2, 0
+
+
+def place(x, y, co, z):
+    zh, zl = z // ZL, z % ZL
+    return (((zl * (YC // 2) + y) * 2 + co) * XS + x) * ZH + zh
+
+
+def z_groups():
+    zs = [(FIRST_Z + i) % (ZH * ZL) for i in range(ZH * ZL)]
+    return [[place(x, y, co, z) for z in zs] for x in range(XS) for y in range(YC // 2) for co in range(2)]
+
+
+def plane_order():
+    return [
+        ((FIRST_X + i) % XS, (FIRST_Y + j) % (YC // 2), (FIRST_CO + k) % 2)
+        for i in range(XS)
+        for j in range(YC // 2)
+        for k in range(2)
+    ]
+
+
+def plane_groups():
+    return [[place(*xyc, z) for xyc in plane_order()] for z in range(ZH * ZL)]
 
 
 def columns_kernel(
@@ -113,32 +141,39 @@
     partner = jnp.where(odd_row == 1, pltpu.roll(turned, 1, 0), pltpu.roll(turned, ZL * SLOTS - 1, 0))
     pairs = ZL * SLOTS // 2
     result = jnp.where(odd_row == lanes >> 6, shifted, partner).astype(jnp.bfloat16).reshape(pairs, 2, LANES)
-    for half in range(ZH):
-        out_ref[half * pairs : (half + 1) * pairs] = result
+    own = SLOTS // 2
+    for g in range(ZH * ZL):
+        z = (FIRST_Z + g) % ZL
+        out_ref[g * own : (g + 1) * own] = result[z * own : (z + 1) * own]
     rows.wait()
 
 
 def order_kernel(data_ref, out_ref):
-    rows = ZL * SLOTS // 2
-    both = jnp.concatenate([data_ref[h * rows : (h + 1) * rows].reshape(2 * rows, LANES) for h in range(ZH)], axis=1)
+    own = SLOTS // 2
+    halves = []
+    for h in range(ZH):
+        at = [(h * ZL + z - FIRST_Z) % (ZH * ZL) * own for z in range(ZL)]
+        halves.append(jnp.concatenate([data_ref[a : a + own] for a in at], axis=0).reshape(ZL * SLOTS, LANES))
+    both = jnp.concatenate(halves, axis=1)
     rows = jnp.dot(order_matrix(), both, preferred_element_type=jnp.float32).astype(jnp.bfloat16)
-    for j in range(YC):
+    for to, (_, y, co) in enumerate(plane_order()):
+        j = y * 2 + co
         for t in range(EXT_C // 2):
             for h in range(ZH):
                 tile = rows[(2 * j + t) * TILE : (2 * j + t + 1) * TILE, h * LANES : (h + 1) * LANES]
-                for x in range(XS):
-                    out_ref[x * YC + j, (t * ZH + h) * TILE : (t * ZH + h + 1) * TILE, :] = tile
+                out_ref[to, (t * ZH + h) * TILE : (t * ZH + h + 1) * TILE, :] = tile
 
 
 def image_kernel(data_ref, table_ref, out_ref):
     window = window_matrix()
     summed = []
+    at_plane = {xyc: i for i, xyc in enumerate(plane_order())}
     for x in range(XS):
         for h in range(ZH):
             slabs = []
             for t in range(EXT_C // 2):
                 at = (t * ZH + h) * TILE
-                slabs.append(jnp.concatenate([data_ref[x * YC + j, at : at + TILE, :] for j in range(YC)], axis=0))
+                slabs.append(jnp.concatenate([data_ref[at_plane[x, j // 2, j % 2], at : at + TILE, :] for j in range(YC)], axis=0))
             summed.append(jnp.dot(window, jnp.concatenate(slabs, axis=1), preferred_element_type=jnp.float32))
     first = lax.broadcasted_iota(jnp.int32, (SUBAP, LANES), 1) < HALF
     logs = []
@@ -194,7 +229,7 @@
         ],
         compiler_params=params,
     )(strip, *(pltpu.with_memory_space_constraint(a, pltpu.HBM) for a in (offsets, spectra, columns, jnp.asarray(row_matrices()))))
-    got = lax.all_to_all(sent.reshape(ZH * ZL, SLOTS // 2, 2, LANES), ("zh", "zl"), 0, 0, tiled=True)
+    got = lax.all_to_all(sent.reshape(ZH * ZL, SLOTS // 2, 2, LANES), AXES, 0, 0, tiled=True, axis_index_groups=z_groups())
     sent = pl.pallas_call(
         order_kernel,
         out_shape=jax.ShapeDtypeStruct((XS * YC, EXT_C // 2 * ZH * TILE, LANES), jnp.bfloat16),
@@ -202,7 +237,7 @@
         out_specs=vmem,
         compiler_params=params,
     )(got.reshape(sent.shape))
-    data = lax.all_to_all(sent, ("x", "y", "co"), 0, 0, tiled=True)
+    data = lax.all_to_all(sent, AXES, 0, 0, tiled=True, axis_index_groups=plane_groups())
     return pl.pallas_call(
         image_kernel,
         out_shape=jax.ShapeDtypeStruct((OWN_R, OWN_C, SUBAP), jnp.float32),

time: 57.3 us -> 50.4 us (0.88)
  blocking collectives: 52.7 us -> 45.8 us
    all_to_all x2, blocking collectives: 52.7 us -> 45.8 us  [the longest x1 26.1 us: body(): lax.all_to_all(sent.reshape(ZH * ZL, SLOTS // 2, 2, LANES), AXES, 0, 0, t...]
where the time goes in v6:
time: 50.4 us; the launch traced here: 50.2 us
  blocking collectives  45.8 us (91%)
  Pallas kernels  4.33 us (9%)
    all_to_all x1, blocking collectives, body(): lax.all_to_all(sent.reshape(ZH * ZL, SLOTS // 2, 2, LANES), AXES, 0, 0, t...  26.1 us
    all_to_all x1, blocking collectives, body(): lax.all_to_all(sent, AXES, 0, 0, tiled=True, axis_index_groups=plane_grou...  19.8 us
    pallas_call x1, Pallas kernels, body(): pl.pallas_call(image_kernel, out_shape=jax.ShapeDtypeStruct((OWN_R, OWN_C...  2.05 us
    pallas_call x1, Pallas kernels, body(): pl.pallas_call(columns_kernel, out_shape=[jax.ShapeDtypeStruct((ZH * ZL *...  2.01 us

profile of v6, /device:TPU:1, one launch (start us, length us, event | category | flops | bytes accessed | tf_op | source)
XLA Modules:
  0.0 50.2 jit_solution(17694676260724813429)
XLA Ops:
  0.0 2.0 %shard_map.46 = (bf16[288,2,128]{2,1,0:T(2,128)(2,1)S(1)}, bf16[272,512]{1,0:T(8,128)(2,1)S(1)}) custom-call(s32[1]{0:T(128)} %bitcast.strip_ref, s32[2]{0:T(128)} %offsets_hbm.1, bf16[2,32,2048]{2,1,0:T(8,128)(2,1)} %spectra_hbm.1, bf16[2,288,1024]{2,1,0:T(8,128)(2,1)} %constant.14.clone.table_hbm, bf16[8,272,512]{2,1,0:T(8,128)(2,1)} %constant.15.clone.tables_hbm), custom_call_target="tpu_custom_call" | custom-call | tf_op jit(solution)/shard_map/pallas_call | solution.py:216
  2.0 26.1 %all_to_all.10 = bf16[16,18,2,128]{3,2,1,0:T(2,128)(2,1)S(1)} all-to-all(bf16[16,18,2,128]{3,2,1,0:T(2,128)(2,1)S(1)} %bitcast.4), channel_id=1, replica_groups={{1,65,129,193,257,321,385,449,0,64,128,192,256,320,384,448},{9,73,137,2..., dimensions={0} | all-to-all | bytes 294912 | tf_op jit(solution)/shard_map/all_to_all | solution.py:232
  28.1 0.3 shard_map.47
  28.4 19.8 %all_to_all.11.data_ref = bf16[32,96,128]{2,1,0:T(8,128)(2,1)S(1)} all-to-all(bf16[32,96,128]{2,1,0:T(8,128)(2,1)S(1)} %shard_map.47), channel_id=1, replica_groups={{36,44,52,60,4,12,20,28,38,46,54,62,6,14,22,30,32,40,48,56,0,8,16,24,34..., dimensions={0} | all-to-all | bytes 1572864 | tf_op jit(solution)/shard_map/all_to_all | solution.py:240
  48.1 2.0 %shard_map.48 = f32[128,4,128]{2,1,0:T(4,128)} custom-call(bf16[32,96,128]{2,1,0:T(8,128)(2,1)S(1)} %all_to_all.11.data_ref, bf16[272,512]{1,0:T(8,128)(2,1)S(1)} %get-tuple-element.8.table_ref), custom_call_target="tpu_custom_call" | custom-call | tf_op jit(solution)/shard_map/pallas_call | solution.py:241

commit v7 on v6

--- a/solution.py
+++ b/solution.py
@@ -35,7 +35,7 @@
 
 
 def column_matrix():
-    n = np.arange(KA)[None, :]
+    n = np.arange(KA // 2)[None, :]
     slot = np.arange(SLOTS)[None, :]
     col = (np.arange(ZL)[:, None] * BLOCK - 1 + slot).reshape(-1, 1)
     valid = np.broadcast_to(slot < BLOCK + 2, (ZL, SLOTS)).reshape(-1, 1) & (col >= 0) & (col < COLS)
@@ -77,8 +77,8 @@
 
 
 AXES = ("zl", "y", "co", "x", "zh")
-FIRST_Z = 8
-FIRST_X, FIRST_Y, FIRST_CO = 2, 2, 0
+Z_ORDER = (11, 12, 13, 14, 15, 0, 1, 2, 3, 4, 5, 6, 7, 8, 9, 10)
+PLANE_ORDER = ((2, 2, 1), (2, 2, 0), (2, 3, 0), (2, 1, 0), (3, 2, 0), (1, 2, 0), (2, 0, 0), (3, 3, 0), (3, 1, 0), (0, 2, 0), (1, 3, 0), (1, 1, 0), (3, 0, 0), (0, 3, 0), (0, 1, 0), (1, 0, 0), (0, 0, 0), (2, 3, 1), (2, 1, 1), (3, 2, 1), (1, 2, 1), (2, 0, 1), (3, 3, 1), (3, 1, 1), (0, 2, 1), (1, 3, 1), (1, 1, 1), (3, 0, 1), (0, 3, 1), (0, 1, 1), (1, 0, 1), (0, 0, 1))
 
 
 def place(x, y, co, z):
@@ -87,21 +87,15 @@
 
 
 def z_groups():
-    zs = [(FIRST_Z + i) % (ZH * ZL) for i in range(ZH * ZL)]
-    return [[place(x, y, co, z) for z in zs] for x in range(XS) for y in range(YC // 2) for co in range(2)]
+    return [[place(x, y, co, z) for z in Z_ORDER] for x in range(XS) for y in range(YC // 2) for co in range(2)]
 
 
 def plane_order():
-    return [
-        ((FIRST_X + i) % XS, (FIRST_Y + j) % (YC // 2), (FIRST_CO + k) % 2)
-        for i in range(XS)
-        for j in range(YC // 2)
-        for k in range(2)
-    ]
+    return PLANE_ORDER
 
 
 def plane_groups():
-    return [[place(*xyc, z) for xyc in plane_order()] for z in range(ZH * ZL)]
+    return [[place(*xyc, z) for xyc in PLANE_ORDER] for z in range(ZH * ZL)]
 
 
 def columns_kernel(
@@ -126,24 +120,23 @@
     im = [spectra_ref[s, :, KA:] for s in range(OWN_S)]
     mixed = None
     for fetch, part in zip(fetches, (0, 1)):
-        if part == 0:
-            stack = jnp.concatenate([re[0], im[0], re[1], im[1]], axis=0)
-        else:
-            stack = jnp.concatenate([-im[0], re[0], -im[1], re[1]], axis=0)
+        sides = (re[0], im[0], re[1], im[1]) if part == 0 else (-im[0], re[0], -im[1], re[1])
+        stack = jnp.concatenate([a[:, : KA // 2] for a in sides] + [a[:, KA // 2 :] for a in sides], axis=0)
         fetch.wait()
         product = lax.dot_general(table_ref[part], stack, (((1,), (1,)), ((), ())), preferred_element_type=jnp.float32)
         mixed = product if mixed is None else mixed + product
+    odd_row = lax.broadcasted_iota(jnp.int32, (ZL * SLOTS, LANES), 0) & 1
+    mixed = mixed[:, :LANES] + jnp.where(odd_row == 1, mixed[:, LANES:], -mixed[:, LANES:])
     lanes = lax.broadcasted_iota(jnp.int32, mixed.shape, 1)
     other = jnp.where((lanes & OWN_K) == 0, pltpu.roll(mixed, LANES - OWN_K, 1), pltpu.roll(mixed, OWN_K, 1))
     shifted = mixed * cosine + other * sine
     turned = pltpu.roll(shifted, HALF, 1)
-    odd_row = lax.broadcasted_iota(jnp.int32, shifted.shape, 0) & 1
     partner = jnp.where(odd_row == 1, pltpu.roll(turned, 1, 0), pltpu.roll(turned, ZL * SLOTS - 1, 0))
     pairs = ZL * SLOTS // 2
     result = jnp.where(odd_row == lanes >> 6, shifted, partner).astype(jnp.bfloat16).reshape(pairs, 2, LANES)
     own = SLOTS // 2
     for g in range(ZH * ZL):
-        z = (FIRST_Z + g) % ZL
+        z = Z_ORDER[g] % ZL
         out_ref[g * own : (g + 1) * own] = result[z * own : (z + 1) * own]
     rows.wait()
 
@@ -152,7 +145,7 @@
     own = SLOTS // 2
     halves = []
     for h in range(ZH):
-        at = [(h * ZL + z - FIRST_Z) % (ZH * ZL) * own for z in range(ZL)]
+        at = [Z_ORDER.index(h * ZL + z) * own for z in range(ZL)]
         halves.append(jnp.concatenate([data_ref[a : a + own] for a in at], axis=0).reshape(ZL * SLOTS, LANES))
     both = jnp.concatenate(halves, axis=1)
     rows = jnp.dot(order_matrix(), both, preferred_element_type=jnp.float32).astype(jnp.bfloat16)
@@ -177,25 +170,19 @@
             summed.append(jnp.dot(window, jnp.concatenate(slabs, axis=1), preferred_element_type=jnp.float32))
     first = lax.broadcasted_iota(jnp.int32, (SUBAP, LANES), 1) < HALF
     logs = []
-    for c in range(EXT_C):
-        at = (c // 2) * LANES
-        lanes = []
+    for t in range(EXT_C // 2):
+        at = t * LANES
+        columns = ([], [])
         for st in range(0, STRIPS, 2):
             a = summed[st][:, at : at + LANES]
             b = summed[st + 1][:, at : at + LANES]
-            if c % 2 == 0:
-                both = jnp.where(first, a, pltpu.roll(b, HALF, 1))
-            else:
-                both = jnp.where(first, pltpu.roll(a, HALF, 1), b)
-            lanes.append(both.astype(jnp.bfloat16))
-        frames = lax.dot_general(
-            table_ref[...],
-            jnp.concatenate(lanes, axis=1),
-            (((1,), (1,)), ((), ())),
-            preferred_element_type=jnp.float32,
-        )
-        re, im = frames[:EXT_R], frames[EXT_R:]
-        logs.append(jnp.log(1.0 + re * re + im * im))
+            columns[0].append(jnp.where(first, a, pltpu.roll(b, HALF, 1)).astype(jnp.bfloat16))
+            columns[1].append(jnp.where(first, pltpu.roll(a, HALF, 1), b).astype(jnp.bfloat16))
+        both = jnp.concatenate([jnp.concatenate(column, axis=1) for column in columns], axis=0)
+        frames = lax.dot_general(table_ref[...], both, (((1,), (1,)), ((), ())), preferred_element_type=jnp.float32)
+        power = frames[:EXT_R] * frames[:EXT_R] + frames[EXT_R:] * frames[EXT_R:]
+        power = jnp.log(1.0 + power)
+        logs += [power[:, :SUBAP], power[:, SUBAP:]]
     for c in range(OWN_C):
         column = logs[c] + logs[c + 1] + logs[c + 2]
         total = column[:OWN_R] + column[1 : OWN_R + 1] + column[2 : OWN_R + 2]

time: 50.4 us -> 49 us (0.972)
  blocking collectives: 45.8 us -> 44.9 us
    all_to_all x1, blocking collectives: 26.1 us -> 25.3 us  [body(): lax.all_to_all(sent.reshape(ZH * ZL, SLOTS // 2, 2, LANES), AXES, 0, 0, t...]
where the time goes in v7:
time: 49 us; the launch traced here: 48.8 us
  blocking collectives  44.9 us (92%)
  Pallas kernels  3.88 us (8%)
    all_to_all x1, blocking collectives, body(): lax.all_to_all(sent.reshape(ZH * ZL, SLOTS // 2, 2, LANES), AXES, 0, 0, t...  25.3 us
    all_to_all x1, blocking collectives, body(): lax.all_to_all(sent, AXES, 0, 0, tiled=True, axis_index_groups=plane_grou...  19.6 us
    pallas_call x1, Pallas kernels, body(): pl.pallas_call(image_kernel, out_shape=jax.ShapeDtypeStruct((OWN_R, OWN_C...  1.91 us
    pallas_call x1, Pallas kernels, body(): pl.pallas_call(columns_kernel, out_shape=[jax.ShapeDtypeStruct((ZH * ZL *...  1.7 us

profile of v7, /device:TPU:1, one launch (start us, length us, event | category | flops | bytes accessed | tf_op | source)
XLA Modules:
  0.0 48.8 jit_solution(882667057538416989)
XLA Ops:
  0.0 1.7 %shard_map.46 = (bf16[288,2,128]{2,1,0:T(2,128)(2,1)S(1)}, bf16[272,512]{1,0:T(8,128)(2,1)S(1)}) custom-call(s32[1]{0:T(128)} %bitcast.strip_ref, s32[2]{0:T(128)} %offsets_hbm.1, bf16[2,32,2048]{2,1,0:T(8,128)(2,1)} %spectra_hbm.1, bf16[2,288,512]{2,1,0:T(8,128)(2,1)} %constant.14.clone.table_hbm, bf16[8,272,512]{2,1,0:T(8,128)(2,1)} %constant.15.clone.tables_hbm), custom_call_target="tpu_custom_call" | custom-call | tf_op jit(solution)/shard_map/pallas_call | solution.py:203
  1.7 25.3 %all_to_all.10 = bf16[16,18,2,128]{3,2,1,0:T(2,128)(2,1)S(1)} all-to-all(bf16[16,18,2,128]{3,2,1,0:T(2,128)(2,1)S(1)} %bitcast.4), channel_id=1, replica_groups={{193,257,321,385,449,0,64,128,192,256,320,384,448,1,65,129},{201,265,32..., dimensions={0} | all-to-all | bytes 294912 | tf_op jit(solution)/shard_map/all_to_all | solution.py:219
  27.0 0.3 shard_map.47
  27.3 19.6 %all_to_all.11.data_ref = bf16[32,96,128]{2,1,0:T(8,128)(2,1)S(1)} all-to-all(bf16[32,96,128]{2,1,0:T(8,128)(2,1)S(1)} %shard_map.47), channel_id=1, replica_groups={{44,36,52,20,38,34,4,54,22,32,50,18,6,48,16,2,0,60,28,46,42,12,62,30,40..., dimensions={0} | all-to-all | bytes 1572864 | tf_op jit(solution)/shard_map/all_to_all | solution.py:227
  46.9 1.9 %shard_map.48 = f32[128,4,128]{2,1,0:T(4,128)} custom-call(bf16[32,96,128]{2,1,0:T(8,128)(2,1)S(1)} %all_to_all.11.data_ref, bf16[272,512]{1,0:T(8,128)(2,1)S(1)} %get-tuple-element.8.table_ref), custom_call_target="tpu_custom_call" | custom-call | tf_op jit(solution)/shard_map/pallas_call | solution.py:228

commit v8 on v7

--- a/solution.py
+++ b/solution.py
@@ -30,7 +30,7 @@
 ZL, YC, XS, ZH = 8, 8, 4, 2
 BLOCK = COLS // ZL
 PAIRS = BLOCK // 2 + 1
-SLOTS = BLOCK + 4
+SLOTS = BLOCK + 2
 TILE = OWN_S * ZL
 
 
@@ -168,7 +168,6 @@
                 at = (t * ZH + h) * TILE
                 slabs.append(jnp.concatenate([data_ref[at_plane[x, j // 2, j % 2], at : at + TILE, :] for j in range(YC)], axis=0))
             summed.append(jnp.dot(window, jnp.concatenate(slabs, axis=1), preferred_element_type=jnp.float32))
-    first = lax.broadcasted_iota(jnp.int32, (SUBAP, LANES), 1) < HALF
     logs = []
     for t in range(EXT_C // 2):
         at = t * LANES
@@ -176,8 +175,9 @@
         for st in range(0, STRIPS, 2):
             a = summed[st][:, at : at + LANES]
             b = summed[st + 1][:, at : at + LANES]
-            columns[0].append(jnp.where(first, a, pltpu.roll(b, HALF, 1)).astype(jnp.bfloat16))
-            columns[1].append(jnp.where(first, pltpu.roll(a, HALF, 1), b).astype(jnp.bfloat16))
+            a, b = a.astype(jnp.bfloat16), b.astype(jnp.bfloat16)
+            columns[0].append(jnp.concatenate([a[:, :HALF], b[:, :HALF]], axis=1))
+            columns[1].append(jnp.concatenate([a[:, HALF:], b[:, HALF:]], axis=1))
         both = jnp.concatenate([jnp.concatenate(column, axis=1) for column in columns], axis=0)
         frames = lax.dot_general(table_ref[...], both, (((1,), (1,)), ((), ())), preferred_element_type=jnp.float32)
         power = frames[:EXT_R] * frames[:EXT_R] + frames[EXT_R:] * frames[EXT_R:]

time: 49 us -> 48.6 us (level)
  no operation moved by 1% of the time
where the time goes in v8:
time: 48.6 us; the launch traced here: 48.4 us
  blocking collectives  44.6 us (92%)
  Pallas kernels  3.83 us (8%)
    all_to_all x1, blocking collectives, body(): lax.all_to_all(sent.reshape(ZH * ZL, SLOTS // 2, 2, LANES), AXES, 0, 0, t...  25 us
    all_to_all x1, blocking collectives, body(): lax.all_to_all(sent, AXES, 0, 0, tiled=True, axis_index_groups=plane_grou...  19.6 us
    pallas_call x1, Pallas kernels, body(): pl.pallas_call(image_kernel, out_shape=jax.ShapeDtypeStruct((OWN_R, OWN_C...  1.88 us
    pallas_call x1, Pallas kernels, body(): pl.pallas_call(columns_kernel, out_shape=[jax.ShapeDtypeStruct((ZH * ZL *...  1.68 us

profile of v8, /device:TPU:1, one launch (start us, length us, event | category | flops | bytes accessed | tf_op | source)
XLA Modules:
  0.0 48.4 jit_solution(4326849853611842691)
XLA Ops:
  0.0 1.7 %shard_map.46 = (bf16[272,2,128]{2,1,0:T(2,128)(2,1)S(1)}, bf16[272,512]{1,0:T(8,128)(2,1)S(1)}) custom-call(s32[1]{0:T(128)} %bitcast.strip_ref, s32[2]{0:T(128)} %offsets_hbm.1, bf16[2,32,2048]{2,1,0:T(8,128)(2,1)} %spectra_hbm.1, bf16[2,272,512]{2,1,0:T(8,128)(2,1)} %constant.14.clone.table_hbm, bf16[8,272,512]{2,1,0:T(8,128)(2,1)} %constant.15.clone.tables_hbm), custom_call_target="tpu_custom_call" | custom-call | tf_op jit(solution)/shard_map/pallas_call | solution.py:203
  1.7 25.0 %all_to_all.10 = bf16[16,17,2,128]{3,2,1,0:T(2,128)(2,1)S(1)} all-to-all(bf16[16,17,2,128]{3,2,1,0:T(2,128)(2,1)S(1)} %bitcast.4), channel_id=1, replica_groups={{193,257,321,385,449,0,64,128,192,256,320,384,448,1,65,129},{201,265,32..., dimensions={0} | all-to-all | bytes 278528 | tf_op jit(solution)/shard_map/all_to_all | solution.py:219
  26.7 0.3 shard_map.47
  27.0 19.6 %all_to_all.11.data_ref = bf16[32,96,128]{2,1,0:T(8,128)(2,1)S(1)} all-to-all(bf16[32,96,128]{2,1,0:T(8,128)(2,1)S(1)} %shard_map.47), channel_id=1, replica_groups={{44,36,52,20,38,34,4,54,22,32,50,18,6,48,16,2,0,60,28,46,42,12,62,30,40..., dimensions={0} | all-to-all | bytes 1572864 | tf_op jit(solution)/shard_map/all_to_all | solution.py:227
  46.5 1.9 %shard_map.48 = f32[128,4,128]{2,1,0:T(4,128)} custom-call(bf16[32,96,128]{2,1,0:T(8,128)(2,1)S(1)} %all_to_all.11.data_ref, bf16[272,512]{1,0:T(8,128)(2,1)S(1)} %get-tuple-element.8.table_ref), custom_call_target="tpu_custom_call" | custom-call | tf_op jit(solution)/shard_map/pallas_call | solution.py:228

commit v9 on v8

--- a/solution.py
+++ b/solution.py
@@ -67,6 +67,13 @@
     lane = lax.broadcasted_iota(jnp.int32, (SUBAP, SUBAP), 1)
     sub = OWN_S * ((lane & (ZL - 1)) * YC + (lane >> 4)) + ((lane >> 3) & 1)
     return jnp.where(((sub - frame) & (SUBAP - 1)) < WIN, 1.0, 0.0).astype(jnp.bfloat16)
+
+
+def background_matrix():
+    source = lax.broadcasted_iota(jnp.int32, (SUBAP, SUBAP), 0)
+    frame = lax.broadcasted_iota(jnp.int32, (SUBAP, SUBAP), 1)
+    mean = jnp.where(((frame - source) & (SUBAP - 1)) < BG, 1.0 / BG, 0.0)
+    return (jnp.where(source == frame, 1.0, 0.0) - mean).astype(jnp.bfloat16)
 
 
 def order_matrix():
@@ -183,14 +190,22 @@
         power = frames[:EXT_R] * frames[:EXT_R] + frames[EXT_R:] * frames[EXT_R:]
         power = jnp.log(1.0 + power)
         logs += [power[:, :SUBAP], power[:, SUBAP:]]
+    filtered = []
     for c in range(OWN_C):
         column = logs[c] + logs[c + 1] + logs[c + 2]
         total = column[:OWN_R] + column[1 : OWN_R + 1] + column[2 : OWN_R + 2]
-        filtered = total * (1.0 / 9.0)
-        back = filtered
-        for step in (1, 2, 4, 8):
-            back = back + pltpu.roll(back, step, 1)
-        out_ref[:, c, :] = filtered - back * (1.0 / BG)
+        filtered.append(total * (1.0 / 9.0))
+    filtered = jnp.concatenate(filtered, axis=0)
+    high = filtered.astype(jnp.bfloat16)
+    low = (filtered - high.astype(jnp.float32)).astype(jnp.bfloat16)
+    weights = background_matrix()
+    result = jnp.dot(
+        jnp.concatenate([high, low], axis=1),
+        jnp.concatenate([weights, weights], axis=0),
+        preferred_element_type=jnp.float32,
+    )
+    for c in range(OWN_C):
+        out_ref[:, c, :] = result[c * OWN_R : (c + 1) * OWN_R]
 
 
 def body(spectra, offsets):

time: 48.6 us -> 48.5 us (level)
  no operation moved by 1% of the time
where the time goes in v9:
time: 48.5 us; the launch traced here: 48.3 us
  blocking collectives  44.6 us (92%)
  Pallas kernels  3.69 us (8%)
    all_to_all x1, blocking collectives, body(): lax.all_to_all(sent.reshape(ZH * ZL, SLOTS // 2, 2, LANES), AXES, 0, 0, t...  25 us
    all_to_all x1, blocking collectives, body(): lax.all_to_all(sent, AXES, 0, 0, tiled=True, axis_index_groups=plane_grou...  19.6 us
    pallas_call x1, Pallas kernels, body(): pl.pallas_call(image_kernel, out_shape=jax.ShapeDtypeStruct((OWN_R, OWN_C...  1.74 us
    pallas_call x1, Pallas kernels, body(): pl.pallas_call(columns_kernel, out_shape=[jax.ShapeDtypeStruct((ZH * ZL *...  1.68 us

profile of v9, /device:TPU:1, one launch (start us, length us, event | category | flops | bytes accessed | tf_op | source)
XLA Modules:
  0.0 48.3 jit_solution(3272517884364702775)
XLA Ops:
  0.0 1.7 %shard_map.46 = (bf16[272,2,128]{2,1,0:T(2,128)(2,1)S(1)}, bf16[272,512]{1,0:T(8,128)(2,1)S(1)}) custom-call(s32[1]{0:T(128)} %bitcast.strip_ref, s32[2]{0:T(128)} %offsets_hbm.1, bf16[2,32,2048]{2,1,0:T(8,128)(2,1)} %spectra_hbm.1, bf16[2,272,512]{2,1,0:T(8,128)(2,1)} %constant.14.clone.table_hbm, bf16[8,272,512]{2,1,0:T(8,128)(2,1)} %constant.15.clone.tables_hbm), custom_call_target="tpu_custom_call" | custom-call | tf_op jit(solution)/shard_map/pallas_call | solution.py:218
  1.7 25.0 %all_to_all.10 = bf16[16,17,2,128]{3,2,1,0:T(2,128)(2,1)S(1)} all-to-all(bf16[16,17,2,128]{3,2,1,0:T(2,128)(2,1)S(1)} %bitcast.4), channel_id=1, replica_groups={{193,257,321,385,449,0,64,128,192,256,320,384,448,1,65,129},{201,265,32..., dimensions={0} | all-to-all | bytes 278528 | tf_op jit(solution)/shard_map/all_to_all | solution.py:234
  26.7 0.3 shard_map.47
  27.0 19.6 %all_to_all.11.data_ref = bf16[32,96,128]{2,1,0:T(8,128)(2,1)S(1)} all-to-all(bf16[32,96,128]{2,1,0:T(8,128)(2,1)S(1)} %shard_map.47), channel_id=1, replica_groups={{44,36,52,20,38,34,4,54,22,32,50,18,6,48,16,2,0,60,28,46,42,12,62,30,40..., dimensions={0} | all-to-all | bytes 1572864 | tf_op jit(solution)/shard_map/all_to_all | solution.py:242
  46.5 1.7 %shard_map.48 = f32[128,4,128]{2,1,0:T(4,128)} custom-call(bf16[32,96,128]{2,1,0:T(8,128)(2,1)S(1)} %all_to_all.11.data_ref, bf16[272,512]{1,0:T(8,128)(2,1)S(1)} %get-tuple-element.8.table_ref), custom_call_target="tpu_custom_call" | custom-call | tf_op jit(solution)/shard_map/pallas_call | solution.py:243

commit v10 on v9

--- a/solution.py
+++ b/solution.py
@@ -84,7 +84,7 @@
 
 
 AXES = ("zl", "y", "co", "x", "zh")
-Z_ORDER = (11, 12, 13, 14, 15, 0, 1, 2, 3, 4, 5, 6, 7, 8, 9, 10)
+Z_ORDER = (10, 11, 9, 12, 8, 13, 7, 14, 6, 15, 5, 0, 4, 1, 3, 2)
 PLANE_ORDER = ((2, 2, 1), (2, 2, 0), (2, 3, 0), (2, 1, 0), (3, 2, 0), (1, 2, 0), (2, 0, 0), (3, 3, 0), (3, 1, 0), (0, 2, 0), (1, 3, 0), (1, 1, 0), (3, 0, 0), (0, 3, 0), (0, 1, 0), (1, 0, 0), (0, 0, 0), (2, 3, 1), (2, 1, 1), (3, 2, 1), (1, 2, 1), (2, 0, 1), (3, 3, 1), (3, 1, 1), (0, 2, 1), (1, 3, 1), (1, 1, 1), (3, 0, 1), (0, 3, 1), (0, 1, 1), (1, 0, 1), (0, 0, 1))
 
 

time: 48.5 us -> 48.1 us (level)
  no operation moved by 1% of the time
where the time goes in v10:
time: 48.1 us; the launch traced here: 48 us
  blocking collectives  44.3 us (92%)
  Pallas kernels  3.69 us (8%)
    all_to_all x1, blocking collectives, body(): lax.all_to_all(sent.reshape(ZH * ZL, SLOTS // 2, 2, LANES), AXES, 0, 0, t...  24.9 us
    all_to_all x1, blocking collectives, body(): lax.all_to_all(sent, AXES, 0, 0, tiled=True, axis_index_groups=plane_grou...  19.4 us
    pallas_call x1, Pallas kernels, body(): pl.pallas_call(image_kernel, out_shape=jax.ShapeDtypeStruct((OWN_R, OWN_C...  1.74 us
    pallas_call x1, Pallas kernels, body(): pl.pallas_call(columns_kernel, out_shape=[jax.ShapeDtypeStruct((ZH * ZL *...  1.68 us

profile of v10, /device:TPU:1, one launch (start us, length us, event | category | flops | bytes accessed | tf_op | source)
XLA Modules:
  0.0 48.0 jit_solution(9991768303177099306)
XLA Ops:
  0.0 1.7 %shard_map.46 = (bf16[272,2,128]{2,1,0:T(2,128)(2,1)S(1)}, bf16[272,512]{1,0:T(8,128)(2,1)S(1)}) custom-call(s32[1]{0:T(128)} %bitcast.strip_ref, s32[2]{0:T(128)} %offsets_hbm.1, bf16[2,32,2048]{2,1,0:T(8,128)(2,1)} %spectra_hbm.1, bf16[2,272,512]{2,1,0:T(8,128)(2,1)} %constant.14.clone.table_hbm, bf16[8,272,512]{2,1,0:T(8,128)(2,1)} %constant.15.clone.tables_hbm), custom_call_target="tpu_custom_call" | custom-call | tf_op jit(solution)/shard_map/pallas_call | solution.py:218
  1.7 24.9 %all_to_all.10 = bf16[16,17,2,128]{3,2,1,0:T(2,128)(2,1)S(1)} all-to-all(bf16[16,17,2,128]{3,2,1,0:T(2,128)(2,1)S(1)} %bitcast.4), channel_id=1, replica_groups={{129,193,65,257,1,321,448,385,384,449,320,0,256,64,192,128},{137,201,73..., dimensions={0} | all-to-all | bytes 278528 | tf_op jit(solution)/shard_map/all_to_all | solution.py:234
  26.6 0.3 shard_map.47
  26.9 19.4 %all_to_all.11.data_ref = bf16[32,96,128]{2,1,0:T(8,128)(2,1)S(1)} all-to-all(bf16[32,96,128]{2,1,0:T(8,128)(2,1)S(1)} %shard_map.47), channel_id=1, replica_groups={{44,36,52,20,38,34,4,54,22,32,50,18,6,48,16,2,0,60,28,46,42,12,62,30,40..., dimensions={0} | all-to-all | bytes 1572864 | tf_op jit(solution)/shard_map/all_to_all | solution.py:242
  46.2 1.7 %shard_map.48 = f32[128,4,128]{2,1,0:T(4,128)} custom-call(bf16[32,96,128]{2,1,0:T(8,128)(2,1)S(1)} %all_to_all.11.data_ref, bf16[272,512]{1,0:T(8,128)(2,1)S(1)} %get-tuple-element.8.table_ref), custom_call_target="tpu_custom_call" | custom-call | tf_op jit(solution)/shard_map/pallas_call | solution.py:243
